TPU v7x, 256 devices: a whole 4x4x8 slice. The times are simulated.
256 devices in a mesh: dp: 16 (over y, x), fsdp: 16 (over z, core).
Axes of the slice: x: 4, y: 4, z: 8, core: 2. Of those that a mesh axis runs over, the one named last changes fastest.
Arguments:
- hidden: bfloat16 [16, 16, 2, 128, 14336], P('dp', 'fsdp'), may hold values from -6 to 6
- cotangent: bfloat16 [16, 16, 2, 128, 1792], P('dp', 'fsdp'), may hold values from -20 to 20
- counts: int32 [16, 16], P('dp', 'fsdp'), may hold values from 0 to 2, as said below
- noise: float32 [14336, 1792], P(('dp', 'fsdp')), may hold values from -224 to 224
Outputs:
- gradient: float32 [14336, 1792], P(('dp', 'fsdp'))
Inputs may be any that keep to these rules, and one draw needn't show every extreme that they name: On every fsdp index, the counts of the first j dp indices sum to j * 1 plus 0 to 1, and the counts of all dp indices sum to exactly 1 times the number of dp indices. A device's examples fill its slots from slot 0.
All inputs are finite; a program needn't handle non-finite values.
Results may differ from a plain program's by a relative error of at most 0.0025.
Values may be sent and summed in bfloat16 or wider, within the bound.
No kernel may reach another device: no remote copies, remote signals or barrier semaphores. Data moves between devices by JAX's collectives and lax.ppermute only.
A program may use at most 128 MiB of HBM per device.

v0:
```python
import math

import jax
import jax.numpy as jnp
from jax import lax
from jax.sharding import PartitionSpec as P

D = 1792
F = 14336
L = 128
BAL = 1
POOL = 2


def clip_weights(hidden_rows, cotangent_matrix_rows, live_slots):
    clipping_threshold = math.sqrt(L * F * D)
    hidden_gram_matrix = jnp.einsum(
        "slf,smf->slm", hidden_rows, hidden_rows, preferred_element_type=jnp.float32
    )
    cotangent_gram_matrix = jnp.einsum(
        "ogj,oij->ogi",
        cotangent_matrix_rows,
        cotangent_matrix_rows,
        preferred_element_type=jnp.float32,
    )
    norm_values = jnp.sqrt(jnp.sum(hidden_gram_matrix * cotangent_gram_matrix, axis=(1, 2)))
    return jnp.where(
        live_slots,
        clipping_threshold / jnp.maximum(norm_values, clipping_threshold),
        jnp.float32(0.0),
    )


def scale_rows(factors, cotangent_matrix_rows):
    return (factors[:, None, None] * cotangent_matrix_rows.astype(jnp.float32)).astype(jnp.bfloat16)


def body(hidden, cotangent, counts, noise):
    pool_hidden = hidden[0, 0]
    pool_cotangent = cotangent[0, 0]
    held_count = counts[0, 0]
    live_slots = jnp.arange(POOL, dtype=jnp.int32) < held_count
    factors = clip_weights(pool_hidden, pool_cotangent, live_slots)
    outgoing = scale_rows(factors, pool_cotangent)
    gathered = lax.all_gather(outgoing, "dp", axis=0, tiled=True)
    blocks = lax.all_to_all(pool_hidden, "dp", split_axis=2, concat_axis=0, tiled=True)
    block_width = blocks.shape[2]
    flat_hidden = blocks.reshape(-1, block_width)
    flat_cotangent = gathered.reshape(-1, gathered.shape[2])
    summed = lax.psum_scatter(
        lax.dot_general(
            flat_hidden,
            flat_cotangent,
            (((0,), (0,)), ((), ())),
            preferred_element_type=jnp.float32,
        ),
        "fsdp",
        scatter_dimension=0,
        tiled=True,
    )
    expected = BAL * lax.axis_size("dp") * lax.axis_size("fsdp")
    return (summed + noise) / expected


def solution(mesh):
    in_specs = (
        P("dp", "fsdp", None, None, None),
        P("dp", "fsdp", None, None, None),
        P("dp", "fsdp"),
        P(("dp", "fsdp"), None),
    )
    out_specs = P(("dp", "fsdp"), None)
    return jax.shard_map(body, mesh=mesh, in_specs=in_specs, out_specs=out_specs, check_vma=False)
```

profile of v0, /device:TPU:32, one launch (start us, length us, event | category | flops | bytes accessed | tf_op | source)
XLA Modules:
  0.0 316.0 jit_solution(3636577716956538434)
XLA Ops:
  6.5 0.0 all-gather.2.cloned.1.call-start
  7.2 18.6 %copy.22 = bf16[1,1,2,128,14336]{3,2,4,1,0:T(2,128)(2,1)} copy(bf16[1,1,2,128,14336]{4,3,2,1,0:T(8,128)(2,1)} %param.4) | data formatting | bytes 14680064 | tf_op args[0]
  25.8 0.0 copy-start
  25.8 8.2 %fusion = f32[2,128,128]{2,1,0:T(8,128)S(1)} fusion(bf16[2,128,14336]{1,0,2:T(2,128)(2,1)} %bitcast.17), kind=kOutput, calls=%fused_computation | convolution fusion | flops 939524096 | bytes 7471104 | tf_op jit(solution)/shard_map/slf,smf->slm/dot_general | solution.py:17
  34.0 0.0 copy-done
  34.0 0.5 fusion.2
  34.5 1.2 multiply_convert_fusion
  35.7 0.0 all-gather.2.cloned.1.call-update
  35.8 0.0 reduce-scatter.4.cloned.1.call-start
  35.8 106.4 %all_to_all.15 = bf16[2,128,14336]{1,0,2:T(2,128)(2,1)S(1)} all-to-all(bf16[2,128,14336]{1,0,2:T(2,128)(2,1)} %bitcast.18), channel_id=1, replica_groups=mesh['dp'=16,'fsdp'=16] {'dp'}, dimensions={2} | all-to-all | bytes 14680064 | tf_op jit(solution)/shard_map/all_to_all | solution.py:46
  142.2 5.6 %copy.25 = bf16[2,128,14336]{1,2,0:T(8,128)(2,1)} copy(bf16[2,128,14336]{1,0,2:T(2,128)(2,1)S(1)} %all_to_all.15) | data formatting | bytes 14680064 | tf_op jit(solution)/shard_map/all_to_all | solution.py:46
  147.8 11.4 %copy.26 = bf16[16,2,128,896]{3,2,1,0:T(8,128)(2,1)} copy(bf16[16,2,128,896]{2,3,0,1:T(8,128)(2,1)} %bitcast.19) | data formatting | bytes 14680064 | tf_op jit(solution)/shard_map/all_to_all | solution.py:46
  159.2 54.4 %all-gather.2.cloned.1.call-done = bf16[32,128,1792]{2,1,0:T(8,128)(2,1)} async-done(((bf16[2,128,1792]{2,1,0:T(8,128)(2,1)}), bf16[32,128,1792]{2,1,0:T(8,128)(2,1)}) %all-gather.2.cloned.1.call-update) | async-done | bytes 14680080 | tf_op jit(solution)/shard_map/all_gather | solution.py:45
  213.6 22.6 %convolution_bitcast_fusion = f32[896,1792]{0,1:T(8,128)} fusion(bf16[4096,1792]{1,0:T(8,128)(2,1)} %bitcast.21, bf16[4096,896]{1,0:T(8,128)(2,1)} %bitcast.20), kind=kOutput, calls=%fused_computation.2 | convolution fusion | flops 13153337344 | bytes 28442624 | tf_op jit(solution)/shard_map/dot_general | solution.py:51
  236.1 0.0 copy-start.1
  236.1 7.9 %copy.28 = f32[896,1792]{1,0:T(8,128)} copy(f32[896,1792]{0,1:T(8,128)} %convolution_bitcast_fusion) | data formatting | bytes 12845056
  244.0 0.0 reduce-scatter.4.cloned.1.call-update
  244.0 63.3 %reduce-scatter.4.cloned.1.call-done = f32[56,1792]{1,0:T(8,128)} async-done(((f32[896,1792]{1,0:T(8,128)}), f32[56,1792]{1,0:T(8,128)}) %reduce-scatter.4.cloned.1.call-update) | async-done | bytes 401424 | tf_op jit(solution)/shard_map/reduce_scatter | solution.py:50
  307.4 0.0 copy-done.1
  307.4 1.8 add_multiply_fusion
  (1 shorter events, 0.0 us)
Async XLA Ops:
  6.5 207.1 %all-gather.2.cloned.1.call-start = ((), (), s32[]{:S(2)}) async-start(), calls=%async_computation.2 | async-start | bytes 15597568 | tf_op jit(solution)/shard_map/all_gather | solution.py:45
  25.8 8.2 %copy-start = (bf16[1,1,2,128,1792]{4,3,2,1,0:T(8,128)(2,1)S(1)}, bf16[1,1,2,128,1792]{4,3,2,1,0:T(8,128)(2,1)}, u32[]{:S(2)}) copy-start(bf16[1,1,2,128,1792]{4,3,2,1,0:T(8,128)(2,1)} %param.5) | copy-start | bytes 2752516
  35.8 271.6 %reduce-scatter.4.cloned.1.call-start = ((), (), s32[]{:S(2)}) async-start(), calls=%async_computation.3 | async-start | bytes 6823936 | tf_op jit(solution)/shard_map/reduce_scatter | solution.py:50
  236.1 71.2 %copy-start.1 = (f32[56,1792]{1,0:T(8,128)S(1)}, f32[56,1792]{1,0:T(8,128)}, u32[]{:S(2)}) copy-start(f32[56,1792]{1,0:T(8,128)} %param.7) | copy-start | bytes 1204228
Sparse Core Ops, SparseCore 0:
  35.9 177.6 all-gather.1
  244.2 63.1 reduce-scatter.3
where the time goes:
time: 321 us; the launch traced here: 316 us
  waiting for transfers between devices  118 us (37%)
  blocking collectives  106 us (33%)
  local copies, waits for them, and re-layouts  43.6 us (14%)
  matrix products  31.2 us (10%)
  between operations  14.1 us (4%)
    all_to_all x1, blocking collectives, body(): lax.all_to_all(pool_hidden, 'dp', split_axis=2, concat_axis=0, tiled=True)  106 us
    reduce_scatter x1, waiting for transfers between devices, body(): lax.psum_scatter(lax.dot_general(flat_hidden, flat_cotangent, (((0,), (0,...  63.3 us
    all_gather x1, waiting for transfers between devices, body(): gathered = lax.all_gather(outgoing, 'dp', axis=0, tiled=True)  54.4 us
    unnamed x6, local copies, waits for them, and re-layouts  26.5 us
    dot_general x1, matrix products, body(): lax.dot_general(flat_hidden, flat_cotangent, (((0,), (0,)), ((), ())), pr...  22.6 us
    all_to_all x2, local copies, waits for them, and re-layouts, body(): lax.all_to_all(pool_hidden, 'dp', split_axis=2, concat_axis=0, tiled=True)  17 us
    dot_general x1, matrix products, clip_weights(): jnp.einsum('slf,smf->slm', hidden_rows, hidden_rows, preferred_element_ty...  8.15 us
  transfers between devices with their start and end apart: 2, of which 2 were waited for; matrix products, arithmetic and copies ran while one was open for 5% of the time, Pallas kernels for 0%

commit v1 on v0

v1 whole, which is shorter than its diff:
```python
import math

import jax
import jax.numpy as jnp
from jax import lax
from jax.experimental import pallas as pl
from jax.experimental.pallas import tpu as pltpu
from jax.sharding import PartitionSpec as P

D = 1792
F = 14336
L = 128
BAL = 1
POOL = 2
N_DP = 16
N_FSDP = 16
CORES = 2
NZ = N_FSDP // CORES
TOK = POOL * L
BLOCK = F // N_DP
ROWS = BLOCK // N_FSDP
LIVE = N_DP * BAL
TILE = 256
QUARTERS = 4
WIDTHS = (1024, 768)
CLIP = math.sqrt(L * F * D)
VMEM = 58 * 2**20


def prepare_kernel(count_ref, hidden_ref, cotangent_ref, blocks_ref, factor_ref, rows_buf, other_buf, gram, sems):
    def load(d):
        return pltpu.make_async_copy(
            hidden_ref.at[:, :, pl.ds(pl.multiple_of(d * BLOCK, L), BLOCK)], rows_buf.at[d], sems.at[0, d]
        )

    def store(d):
        return pltpu.make_async_copy(rows_buf.at[d], blocks_ref.at[d], sems.at[1, d])

    second = pltpu.make_async_copy(cotangent_ref, other_buf, sems.at[2, 0])
    for d in range(N_DP):
        load(d).start()
    second.start()
    gram[...] = jnp.zeros_like(gram)

    def step(d, carry):
        load(d).wait()
        store(d).start()
        rows = rows_buf[d].reshape(TOK, BLOCK)
        gram[...] += lax.dot_general(
            rows, rows, (((1,), (1,)), ((), ())), preferred_element_type=jnp.float32
        )
        return carry

    lax.fori_loop(0, N_DP, step, 0)
    second.wait()
    held = count_ref[0, 0]
    rows = other_buf[...].reshape(TOK, D)
    other = lax.dot_general(rows, rows, (((1,), (1,)), ((), ())), preferred_element_type=jnp.float32)
    both = gram[...] * other
    lane = lax.broadcasted_iota(jnp.int32, (8, L), 1)
    factors = jnp.zeros((8, L), jnp.float32)
    for s in range(POOL):
        span = slice(s * L, (s + 1) * L)
        squared = jnp.sum(both[span, span], axis=(0, 1), keepdims=True)
        norm = jnp.sqrt(jnp.maximum(squared, 0.0))
        factor = CLIP / jnp.maximum(norm, CLIP)
        factor = jnp.where(s < held, factor, jnp.zeros_like(factor))
        factors = jnp.where(lane == s, factor, factors)
    for d in range(N_DP):
        factor_ref[d] = factors
    for d in range(N_DP):
        store(d).wait()


def prepare(hidden, cotangent, held):
    anywhere = pl.BlockSpec(memory_space=pl.ANY)
    whole = pl.BlockSpec(memory_space=pltpu.VMEM)
    return pl.pallas_call(
        prepare_kernel,
        in_specs=[pl.BlockSpec(memory_space=pltpu.SMEM), anywhere, anywhere],
        out_specs=[anywhere, whole],
        out_shape=[
            jax.ShapeDtypeStruct((N_DP, POOL, L, BLOCK), jnp.bfloat16),
            jax.ShapeDtypeStruct((N_DP, 8, L), jnp.float32),
        ],
        scratch_shapes=[
            pltpu.VMEM((N_DP, POOL, L, BLOCK), jnp.bfloat16),
            pltpu.VMEM((POOL, L, D), jnp.bfloat16),
            pltpu.VMEM((TOK, TOK), jnp.float32),
            pltpu.SemaphoreType.DMA((3, N_DP)),
        ],
        compiler_params=pltpu.CompilerParams(vmem_limit_bytes=VMEM),
        cost_estimate=pl.CostEstimate(
            flops=2 * TOK * L * F, bytes_accessed=4 * TOK * F, transcendentals=0
        ),
        name="prepare",
    )(held, hidden, cotangent)


def turn_kernel(place_ref, blocks_ref, out_ref):
    out_ref[...] = blocks_ref[0].T


def turn(place, blocks):
    return pl.pallas_call(
        turn_kernel,
        grid_spec=pltpu.PrefetchScalarGridSpec(
            num_scalar_prefetch=1,
            grid=(LIVE,),
            in_specs=[
                pl.BlockSpec(
                    (1, L, BLOCK), lambda e, place_ref: (place_ref[e] // POOL, place_ref[e] % POOL, 0)
                )
            ],
            out_specs=pl.BlockSpec((BLOCK, L), lambda e, place_ref: (0, e)),
        ),
        out_shape=jax.ShapeDtypeStruct((BLOCK, LIVE * L), jnp.bfloat16),
        compiler_params=pltpu.CompilerParams(vmem_limit_bytes=VMEM),
        cost_estimate=pl.CostEstimate(flops=0, bytes_accessed=4 * LIVE * L * BLOCK, transcendentals=0),
        name="turn",
    )(place, blocks)


def product_kernel(core_ref, factor_ref, turned_ref, *refs):
    quarters, out_refs, (weighted, total) = refs[:QUARTERS], refs[QUARTERS:-2], refs[-2:]
    for q, ref in enumerate(quarters):
        for k in range(LIVE // QUARTERS):
            e = q * (LIVE // QUARTERS) + k
            rows = ref[k * L : (k + 1) * L, :].astype(jnp.float32)
            weighted[e * L : (e + 1) * L, :] = (factor_ref[e] * rows).astype(jnp.bfloat16)
    total[...] = jnp.dot(turned_ref[...], weighted[...], preferred_element_type=jnp.float32)
    core = core_ref[0]
    start = 0
    for c, width in enumerate(WIDTHS):
        end = start + width // TILE

        @pl.when((pl.program_id(0) >= start) & (pl.program_id(0) < end))
        def _(keep_ref=out_refs[2 * c], send_ref=out_refs[2 * c + 1]):
            for z in range(NZ):
                base = z * CORES * ROWS
                mine = pl.multiple_of(base + core * ROWS, 8)
                others = pl.multiple_of(base + (1 - core) * ROWS, 8)
                keep_ref[z] = total[pl.ds(mine, ROWS), :]
                send_ref[z] = total[pl.ds(others, ROWS), :]

        start = end


def product(core, factors, turned, cotangents):
    scalars = pl.BlockSpec(memory_space=pltpu.SMEM)
    out_specs, out_shape = [], []
    start = 0
    for width in WIDTHS:
        tiles = width // TILE

        def at(i, start=start, tiles=tiles):
            return (0, 0, jnp.clip(i - start, 0, tiles - 1))

        out_specs += [pl.BlockSpec((NZ, ROWS, TILE), at)] * 2
        out_shape += [jax.ShapeDtypeStruct((NZ, ROWS, width), jnp.float32)] * 2
        start += tiles
    return pl.pallas_call(
        product_kernel,
        grid=(D // TILE,),
        in_specs=[scalars, scalars, pl.BlockSpec((BLOCK, LIVE * L), lambda i: (0, 0))]
        + [
            pl.BlockSpec((LIVE * L // QUARTERS, TILE), lambda i, q=q: (q, i)) for q in range(QUARTERS)
        ],
        out_specs=out_specs,
        out_shape=out_shape,
        scratch_shapes=[
            pltpu.VMEM((LIVE * L, TILE), jnp.bfloat16),
            pltpu.VMEM((BLOCK, TILE), jnp.float32),
        ],
        compiler_params=pltpu.CompilerParams(vmem_limit_bytes=VMEM),
        cost_estimate=pl.CostEstimate(
            flops=2 * LIVE * L * BLOCK * D, bytes_accessed=24 * 2**20, transcendentals=0
        ),
        name="product",
    )(core, factors, turned, *[cotangents] * QUARTERS)


def around_z(step):
    return [(i, (i + step * CORES) % N_FSDP) for i in range(N_FSDP)]


def other_core(send):
    return lax.ppermute(send, "fsdp", [(i, i ^ 1) for i in range(N_FSDP)])


def reduce_begin(keep, got):
    z = lax.axis_index("fsdp") // CORES

    def own(offset):
        at = (z + offset) % NZ
        return lax.dynamic_index_in_dim(keep, at, 0, False) + lax.dynamic_index_in_dim(got, at, 0, False)

    half = keep.shape[2] // 2
    far = own(NZ // 2)
    up = lax.ppermute(far[:, :half], "fsdp", around_z(1))
    down = lax.ppermute(far[:, half:], "fsdp", around_z(-1))
    up = jnp.concatenate([up, jnp.zeros_like(up)], 1) + own(NZ // 2 - 1)
    down = jnp.concatenate([jnp.zeros_like(down), down], 1) + own(1 - NZ // 2)
    return own, up, down


def reduce_step(own, up, down, offset):
    up = lax.ppermute(up, "fsdp", around_z(1))
    down = lax.ppermute(down, "fsdp", around_z(-1))
    if offset:
        return up + own(offset), down + own(-offset)
    return up + down + own(0)


def across_dp(value):
    return lax.all_to_all(value, "dp", split_axis=0, concat_axis=0, tiled=True)


def body(hidden, cotangent, counts, noise):
    me = lax.axis_index("dp")
    hidden, cotangent = hidden[0, 0], cotangent[0, 0]
    last = lax.dynamic_index_in_dim(cotangent, jnp.clip(counts[0, 0] - 1, 0, POOL - 1), 0, False)
    last, hidden, counts = lax.optimization_barrier((last, hidden, counts))
    passed = lax.ppermute(last, "dp", [(i, (i + 1) % N_DP) for i in range(N_DP)])
    held = across_dp(jnp.broadcast_to(counts[:, :, None], (N_DP, 8, L)))[:, 0, 0]
    blocks, factors = prepare(hidden, cotangent, counts)

    index = jnp.arange(N_DP, dtype=jnp.int32)
    before = jnp.sum(jnp.where(index[None, :] < index[:, None], held[None, :], 0), axis=1)
    left = jnp.sum(jnp.where(index[None, :] == index[:, None] - 1, held[None, :], 0), axis=1)
    shifted = before > index * BAL
    place = jnp.where(
        shifted,
        jnp.maximum(index - 1, 0) * POOL + jnp.clip(left - 1, 0, POOL - 1),
        index * POOL,
    )
    mine_shifted = jnp.sum(jnp.where(index == me, shifted.astype(jnp.int32), 0)) > 0
    chosen = jnp.where(mine_shifted, passed, cotangent[0])

    chosen, blocks, place, factors = lax.optimization_barrier((chosen, blocks, place, factors))
    cotangents = lax.all_gather(chosen, "dp", axis=0, tiled=True)
    blocks = across_dp(blocks.reshape(N_DP, TOK, BLOCK))
    blocks, factors, place = lax.optimization_barrier((blocks, factors, place))
    factors = across_dp(factors)[:, 0, :POOL].reshape(-1)
    factors = jnp.sum(
        jnp.where(place[:, None] == jnp.arange(N_DP * POOL)[None, :], factors[None, :], 0.0), axis=1
    )
    turned = turn(place, blocks)
    core = (lax.axis_index("fsdp") % CORES).astype(jnp.int32).reshape(1)
    core, factors, turned, cotangents = lax.optimization_barrier((core, factors, turned, cotangents))
    chunks = product(core, factors, turned, cotangents)
    parts = [reduce_begin(keep, other_core(send)) for keep, send in zip(chunks[::2], chunks[1::2])]
    for offset in (2, 1, 0):
        sums = []
        for own, up, down in parts:
            sums.append(reduce_step(own, up, down, offset))
        parts = [(own, *moved) for (own, _, _), moved in zip(parts, sums)] if offset else sums
    return (jnp.concatenate(parts, 1) + noise) / (N_DP * N_FSDP * BAL)


def solution(mesh):
    in_specs = (
        P("dp", "fsdp", None, None, None),
        P("dp", "fsdp", None, None, None),
        P("dp", "fsdp"),
        P(("dp", "fsdp"), None),
    )
    out_specs = P(("dp", "fsdp"), None)
    return jax.shard_map(body, mesh=mesh, in_specs=in_specs, out_specs=out_specs, check_vma=False)
```

time: 321 us -> 234 us (0.73); the launches traced: 316 us -> 233 us
  waiting for transfers between devices: 118 us -> 35.7 us
  local copies, waits for them, and re-layouts: 43.6 us -> 2.92 us
  starting transfers between devices: 0.04 us -> 37 us
  Pallas kernels: 0 us -> 33.2 us
  matrix products: 31.2 us -> 0 us
  other arithmetic: 3.03 us -> 12.7 us
  blocking collectives: 106 us -> 96.6 us
    reduce_scatter x1 -> x0, waiting for transfers between devices: 63.3 us -> none  [body(): lax.psum_scatter(lax.dot_general(flat_hidden, flat_cotangent, (((0,), (0,...]
    all_gather x1, waiting for transfers between devices: 54.4 us -> 13.5 us  [body(): cotangents = lax.all_gather(chosen, 'dp', axis=0, tiled=True)]
    pallas_call x0 -> x3, Pallas kernels: none -> 33.2 us  [the longest x1 13.3 us: product(): pl.pallas_call(product_kernel, grid=(D // TILE,), in_specs=[scalars, scal...]
    dot_general x3 -> x0, matrix products: 31.2 us -> none  [the longest x1 22.6 us: body(): lax.dot_general(flat_hidden, flat_cotangent, (((0,), (0,)), ((), ())), pr...]
    unnamed x6 -> x14, local copies, waits for them, and re-layouts: 26.5 us -> 0.03 us
    ppermute x0 -> x19, starting transfers between devices: none -> 26.5 us  [the longest x6 15.2 us: reduce_step(): up = lax.ppermute(up, 'fsdp', around_z(1))]
    ppermute x0 -> x19, waiting for transfers between devices: none -> 22.2 us  [the longest x6 6.92 us: reduce_step(): up = lax.ppermute(up, 'fsdp', around_z(1))]
    all_to_all x2 -> x0, local copies, waits for them, and re-layouts: 17 us -> none  [body(): lax.all_to_all(pool_hidden, 'dp', split_axis=2, concat_axis=0, tiled=True)]
  transfers between devices with their start and end apart: 2 -> 22, of which waited for: 2 -> 10; matrix products, arithmetic and copies ran while one was open for 5% -> 5% of each run, Pallas kernels for 0% -> 9%
where the time goes in v1:
time: 234 us; the launch traced here: 233 us
  blocking collectives  96.6 us (41%)
  starting transfers between devices  37 us (16%)
  waiting for transfers between devices  35.7 us (15%)
  Pallas kernels  33.2 us (14%)
  between operations  14.9 us (6%)
  other arithmetic  12.7 us (5%)
  local copies, waits for them, and re-layouts  2.92 us (1%)
    all_to_all x1, blocking collectives, across_dp(): return lax.all_to_all(value, 'dp', split_axis=0, concat_axis=0, tiled=True)  96.6 us
    ppermute x6, starting transfers between devices, reduce_step(): up = lax.ppermute(up, 'fsdp', around_z(1))  15.2 us
    all_gather x1, waiting for transfers between devices, body(): cotangents = lax.all_gather(chosen, 'dp', axis=0, tiled=True)  13.5 us
    pallas_call x1, Pallas kernels, product(): pl.pallas_call(product_kernel, grid=(D // TILE,), in_specs=[scalars, scal...  13.3 us
    pallas_call x1, Pallas kernels, turn(): pl.pallas_call(turn_kernel, grid_spec=pltpu.PrefetchScalarGridSpec(num_sc...  11.7 us
    all_to_all x2, starting transfers between devices, across_dp(): return lax.all_to_all(value, 'dp', split_axis=0, concat_axis=0, tiled=True)  10.5 us
    pallas_call x1, Pallas kernels, prepare(): pl.pallas_call(prepare_kernel, in_specs=[pl.BlockSpec(memory_space=pltpu....  8.14 us
    ppermute x6, waiting for transfers between devices, reduce_step(): up = lax.ppermute(up, 'fsdp', around_z(1))  6.92 us
  transfers between devices with their start and end apart: 22, of which 10 were waited for; matrix products, arithmetic and copies ran while one was open for 5% of the time, Pallas kernels for 9%

profile of v1, /device:TPU:32, one launch (start us, length us, event | category | flops | bytes accessed | tf_op | source)
XLA Modules:
  0.0 233.1 jit_solution(7384297991813784359)
XLA Ops:
  7.8 7.0 %all-to-all-start = ((s32[16,8,128]{2,1,0:T(8,128)}), s32[16,8,128]{2,1,0:T(8,128)S(1)}, u32[]{:S(2)}, u32[]{:S(2)}) async-start(s32[16,8,128]{2,1,0:T(8,128)} %broadcast_in_dim.51), calls=%async_computation | async-start | bytes 131072 | tf_op jit(solution)/shard_map/all_to_all | solution.py:216
  16.0 2.0 collective-permute-start
  18.0 8.1 %prepare.1 = (bf16[16,2,128,896]{3,2,1,0:T(8,128)(2,1)}, f32[16,8,128]{2,1,0:T(8,128)}) custom-call(s32[1,1]{1,0:T(1,128)} %copy.5.count_ref, bf16[2,128,14336]{2,1,0:T(8,128)(2,1)} %bitcast.44, bf16[2,128,1792]{2,1,0:T(8,128)(2,1)} %bitcast.45), custom_call_target="tpu_custom_call" | custom-call | flops 939524096 | bytes 14680064 | tf_op jit(solution)/shard_map/prepare/pallas_call | solution.py:78
  28.7 3.1 %collective-permute-done = bf16[128,1792]{1,0:T(8,128)(2,1)S(1)} collective-permute-done((bf16[128,1792]{1,0:T(8,128)(2,1)S(1)}, bf16[128,1792]{1,0:T(8,128)(2,1)S(1)}, u32[]{:S(2)}, u32[]{:S(2)}) %collective-permute-start) | collective-permute-done | bytes 458784 | tf_op jit(solution)/shard_map/ppermute | solution.py:224
  32.6 96.6 %all_to_all.15.blocks_ref = bf16[16,256,896]{2,1,0:T(8,128)(2,1)} all-to-all(bf16[16,256,896]{2,1,0:T(8,128)(2,1)} %bitcast.43), channel_id=1, replica_groups=mesh['dp'=16,'fsdp'=16] {'dp'}, dimensions={0} | all-to-all | bytes 14680064 | tf_op jit(solution)/shard_map/all_to_all | solution.py:216
  129.2 3.5 %all-to-all-start.2 = ((f32[16,8,128]{2,1,0:T(8,128)}), f32[16,8,128]{2,1,0:T(8,128)S(1)}, u32[]{:S(2)}, u32[]{:S(2)}) async-start(f32[16,8,128]{2,1,0:T(8,128)} %get-tuple-element.34), calls=%async_computation.2 | async-start | bytes 131072 | tf_op jit(solution)/shard_map/all_to_all | solution.py:216
  132.8 11.7 %turn.1.turned_ref = bf16[896,2048]{1,0:T(8,128)(2,1)} custom-call(s32[16]{0:T(128)} %get-tuple-element.33.place_ref, bf16[16,256,896]{2,1,0:T(8,128)(2,1)} %all_to_all.15.blocks_ref), custom_call_target="tpu_custom_call" | custom-call | bytes 7340032 | tf_op jit(solution)/shard_map/turn/pallas_call | solution.py:105
  145.3 13.5 %all-gather.2.cloned.1.call-done.refs_0_.refs_1_.refs_2_.refs_3_ = bf16[2048,1792]{1,0:T(8,128)(2,1)} async-done(((bf16[128,1792]{1,0:T(8,128)(2,1)}), bf16[2048,1792]{1,0:T(8,128)(2,1)}) %all-gather.2.cloned.1.call-update) | async-done | bytes 7340048 | tf_op jit(solution)/shard_map/all_gather | solution.py:241
  158.7 13.3 %product.1 = (f32[8,56,1024]{2,1,0:T(8,128)}, f32[8,56,1024]{2,1,0:T(8,128)}, f32[8,56,768]{2,1,0:T(8,128)}, f32[8,56,768]{2,1,0:T(8,128)}) custom-call(s32[1]{0:T(128)} %bitcast.core_ref, f32[16]{0:T(128)} %select_reduce_fusion.factor_ref, bf16[896,2048]{1,0:T(8,128)(2,1)} %turn.1.turned_ref, ...), custom_call_target="tpu_custom_call" | custom-call | flops 6576668672 | bytes 25165824 | tf_op jit(solution)/shard_map/product/pallas_call | solution.py:162
  172.7 5.5 %collective-permute-done.10 = f32[8,56,768]{2,1,0:T(8,128)S(1)} collective-permute-done((f32[8,56,768]{2,1,0:T(8,128)}, f32[8,56,768]{2,1,0:T(8,128)S(1)}, u32[]{:S(2)}, u32[]{:S(2)}) %collective-permute-start.10) | collective-permute-done | bytes 1376288 | tf_op jit(solution)/shard_map/ppermute | solution.py:188
  179.3 1.7 collective-permute-start.11
  183.2 1.6 collective-permute-start.2
  184.8 2.0 collective-permute-start.6
  186.8 2.0 bitcast_add_fusion.10
  188.7 1.7 collective-permute-start.12
  193.4 2.1 collective-permute-start.3
  197.3 2.9 %collective-permute-start.13 = (f32[56,768]{1,0:T(8,128)S(1)}, f32[56,768]{1,0:T(8,128)S(1)}, u32[]{:S(2)}, u32[]{:S(2)}) collective-permute-start(f32[56,768]{1,0:T(8,128)S(1)} %get-tuple-element.56), channel_id=1, source_target_pairs={{0,2},{1,3},{2,4},{3,5},{4,6},{5,7},{6,8},{7,9},{8,10},{9,11},{10,... | collective-permute-start | bytes 516104 | tf_op jit(solution)/shard_map/ppermute | solution.py:208
  200.4 2.7 %collective-permute-done.3 = f32[56,1024]{1,0:T(8,128)S(1)} collective-permute-done((f32[56,1024]{1,0:T(8,128)S(1)}, f32[56,1024]{1,0:T(8,128)S(1)}, u32[]{:S(2)}, u32[]{:S(2)}) %collective-permute-start.3) | collective-permute-done | bytes 229408 | tf_op jit(solution)/shard_map/ppermute | solution.py:208
  204.9 2.9 %collective-permute-start.4 = (f32[56,1024]{1,0:T(8,128)S(1)}, f32[56,1024]{1,0:T(8,128)S(1)}, u32[]{:S(2)}, u32[]{:S(2)}) collective-permute-start(f32[56,1024]{1,0:T(8,128)S(1)} %get-tuple-element.50), channel_id=1, source_target_pairs={{0,2},{1,3},{2,4},{3,5},{4,6},{5,7},{6,8},{7,9},{8,10},{9,11},{10,... | collective-permute-start | bytes 688136 | tf_op jit(solution)/shard_map/ppermute | solution.py:208
  207.9 3.5 %collective-permute-start.14 = (f32[56,768]{1,0:T(8,128)S(1)}, f32[56,768]{1,0:T(8,128)S(1)}, u32[]{:S(2)}, u32[]{:S(2)}) collective-permute-start(f32[56,768]{1,0:T(8,128)S(1)} %get-tuple-element.54), channel_id=1, source_target_pairs={{0,2},{1,3},{2,4},{3,5},{4,6},{5,7},{6,8},{7,9},{8,10},{9,11},{10,... | collective-permute-start | bytes 516104 | tf_op jit(solution)/shard_map/ppermute | solution.py:208
  211.7 3.5 %collective-permute-done.8 = f32[56,1024]{1,0:T(8,128)S(1)} collective-permute-done((f32[56,1024]{1,0:T(8,128)S(1)}, f32[56,1024]{1,0:T(8,128)S(1)}, u32[]{:S(2)}, u32[]{:S(2)}) %collective-permute-start.8) | collective-permute-done | bytes 229408 | tf_op jit(solution)/shard_map/ppermute | solution.py:209
  216.3 2.1 collective-permute-start.5
  218.5 3.9 %collective-permute-done.5 = f32[56,1024]{1,0:T(8,128)S(1)} collective-permute-done((f32[56,1024]{1,0:T(8,128)S(1)}, f32[56,1024]{1,0:T(8,128)S(1)}, u32[]{:S(2)}, u32[]{:S(2)}) %collective-permute-start.5) | collective-permute-done | bytes 229408 | tf_op jit(solution)/shard_map/ppermute | solution.py:208
  222.4 2.0 collective-permute-done.9
  (62 shorter events, 19.3 us)
Async XLA Ops:
  7.8 18.3 %all-to-all-start = ((s32[16,8,128]{2,1,0:T(8,128)}), s32[16,8,128]{2,1,0:T(8,128)S(1)}, u32[]{:S(2)}, u32[]{:S(2)}) async-start(s32[16,8,128]{2,1,0:T(8,128)} %broadcast_in_dim.51), calls=%async_computation | async-start | bytes 131072 | tf_op jit(solution)/shard_map/all_to_all | solution.py:216
  14.9 143.9 %all-gather.2.cloned.1.call-start = ((), (), s32[]{:S(2)}) async-start(), calls=%async_computation.3 | async-start | bytes 7798784 | tf_op jit(solution)/shard_map/all_gather | solution.py:241
  16.0 15.8 %collective-permute-start = (bf16[128,1792]{1,0:T(8,128)(2,1)S(1)}, bf16[128,1792]{1,0:T(8,128)(2,1)S(1)}, u32[]{:S(2)}, u32[]{:S(2)}) collective-permute-start(bf16[128,1792]{1,0:T(8,128)(2,1)S(1)} %dynamic-slice_bitcast_fusion), channel_id=1, source_target_pairs={{0,16},{16,32},{32,48},{48,64},{64,80},{80,96},{96,112},{112,128},... | collective-permute-start | bytes 1376264 | tf_op jit(solution)/shard_map/ppermute | solution.py:224
  129.2 15.2 %all-to-all-start.2 = ((f32[16,8,128]{2,1,0:T(8,128)}), f32[16,8,128]{2,1,0:T(8,128)S(1)}, u32[]{:S(2)}, u32[]{:S(2)}) async-start(f32[16,8,128]{2,1,0:T(8,128)} %get-tuple-element.34), calls=%async_computation.2 | async-start | bytes 131072 | tf_op jit(solution)/shard_map/all_to_all | solution.py:216
  172.1 19.9 %copy-start.1 = (f32[8,56,1024]{2,1,0:T(8,128)S(1)}, f32[8,56,1024]{2,1,0:T(8,128)}, u32[]{:S(2)}) copy-start(f32[8,56,1024]{2,1,0:T(8,128)} %get-tuple-element.41) | copy-start | bytes 5505028
  172.1 9.3 %collective-permute-start.1 = (f32[8,56,1024]{2,1,0:T(8,128)}, f32[8,56,1024]{2,1,0:T(8,128)}, u32[]{:S(2)}, u32[]{:S(2)}) collective-permute-start(f32[8,56,1024]{2,1,0:T(8,128)} %get-tuple-element.42), channel_id=1, source_target_pairs={{0,1},{1,0},{2,3},{3,2},{4,5},{5,4},{6,7},{7,6},{8,9},{9,8},{10,11... | collective-permute-start | bytes 5505032 | tf_op jit(solution)/shard_map/ppermute | solution.py:188
  172.2 5.9 %collective-permute-start.10 = (f32[8,56,768]{2,1,0:T(8,128)}, f32[8,56,768]{2,1,0:T(8,128)S(1)}, u32[]{:S(2)}, u32[]{:S(2)}) collective-permute-start(f32[8,56,768]{2,1,0:T(8,128)} %get-tuple-element.44), channel_id=1, source_target_pairs={{0,1},{1,0},{2,3},{3,2},{4,5},{5,4},{6,7},{7,6},{8,9},{9,8},{10,11... | collective-permute-start | bytes 4128776 | tf_op jit(solution)/shard_map/ppermute | solution.py:188
  179.3 7.5 %collective-permute-start.11 = (f32[56,384]{1,0:T(8,128)S(1)}, f32[56,384]{1,0:T(8,128)S(1)}, u32[]{:S(2)}, u32[]{:S(2)}) collective-permute-start(f32[56,384]{1,0:T(8,128)S(1)} %get-tuple-element.62), channel_id=1, source_target_pairs={{0,2},{1,3},{2,4},{3,5},{4,6},{5,7},{6,8},{7,9},{8,10},{9,11},{10,... | collective-permute-start | bytes 258056 | tf_op jit(solution)/shard_map/ppermute | solution.py:200
  181.0 5.8 %collective-permute-start.15 = (f32[56,384]{1,0:T(8,128)S(1)}, f32[56,384]{1,0:T(8,128)S(1)}, u32[]{:S(2)}, u32[]{:S(2)}) collective-permute-start(f32[56,384]{1,0:T(8,128)S(1)} %get-tuple-element.61), channel_id=1, source_target_pairs={{0,14},{1,15},{2,0},{3,1},{4,2},{5,3},{6,4},{7,5},{8,6},{9,7},{10,... | collective-permute-start | bytes 258056 | tf_op jit(solution)/shard_map/ppermute | solution.py:201
  182.5 14.8 %copy-start.2 = (f32[8,56,768]{2,1,0:T(8,128)S(1)}, f32[8,56,768]{2,1,0:T(8,128)}, u32[]{:S(2)}) copy-start(f32[8,56,768]{2,1,0:T(8,128)} %get-tuple-element.43) | copy-start | bytes 4128772
  183.2 8.8 %collective-permute-start.2 = (f32[56,512]{1,0:T(8,128)}, f32[56,512]{1,0:T(8,128)}, u32[]{:S(2)}, u32[]{:S(2)}) collective-permute-start(f32[56,512]{1,0:T(8,128)} %get-tuple-element.60), channel_id=1, source_target_pairs={{0,2},{1,3},{2,4},{3,5},{4,6},{5,7},{6,8},{7,9},{8,10},{9,11},{10,... | collective-permute-start | bytes 344072 | tf_op jit(solution)/shard_map/ppermute | solution.py:200
  184.8 7.2 %collective-permute-start.6 = (f32[56,512]{1,0:T(8,128)}, f32[56,512]{1,0:T(8,128)}, u32[]{:S(2)}, u32[]{:S(2)}) collective-permute-start(f32[56,512]{1,0:T(8,128)} %get-tuple-element.59), channel_id=1, source_target_pairs={{0,14},{1,15},{2,0},{3,1},{4,2},{5,3},{6,4},{7,5},{8,6},{9,7},{10,... | collective-permute-start | bytes 344072 | tf_op jit(solution)/shard_map/ppermute | solution.py:201
  188.7 8.0 %collective-permute-start.12 = (f32[56,768]{1,0:T(8,128)}, f32[56,768]{1,0:T(8,128)S(1)}, u32[]{:S(2)}, u32[]{:S(2)}) collective-permute-start(f32[56,768]{1,0:T(8,128)} %get-tuple-element.58), channel_id=1, source_target_pairs={{0,2},{1,3},{2,4},{3,5},{4,6},{5,7},{6,8},{7,9},{8,10},{9,11},{10,... | collective-permute-start | bytes 516104 | tf_op jit(solution)/shard_map/ppermute | solution.py:208
  190.5 6.7 %collective-permute-start.16 = (f32[56,768]{1,0:T(8,128)}, f32[56,768]{1,0:T(8,128)S(1)}, u32[]{:S(2)}, u32[]{:S(2)}) collective-permute-start(f32[56,768]{1,0:T(8,128)} %get-tuple-element.57), channel_id=1, source_target_pairs={{0,14},{1,15},{2,0},{3,1},{4,2},{5,3},{6,4},{7,5},{8,6},{9,7},{10,... | collective-permute-start | bytes 516104 | tf_op jit(solution)/shard_map/ppermute | solution.py:209
  193.4 9.7 %collective-permute-start.3 = (f32[56,1024]{1,0:T(8,128)S(1)}, f32[56,1024]{1,0:T(8,128)S(1)}, u32[]{:S(2)}, u32[]{:S(2)}) collective-permute-start(f32[56,1024]{1,0:T(8,128)S(1)} %get-tuple-element.52), channel_id=1, source_target_pairs={{0,2},{1,3},{2,4},{3,5},{4,6},{5,7},{6,8},{7,9},{8,10},{9,11},{10,... | collective-permute-start | bytes 688136 | tf_op jit(solution)/shard_map/ppermute | solution.py:208
  195.5 8.3 %collective-permute-start.7 = (f32[56,1024]{1,0:T(8,128)S(1)}, f32[56,1024]{1,0:T(8,128)S(1)}, u32[]{:S(2)}, u32[]{:S(2)}) collective-permute-start(f32[56,1024]{1,0:T(8,128)S(1)} %get-tuple-element.51), channel_id=1, source_target_pairs={{0,14},{1,15},{2,0},{3,1},{4,2},{5,3},{6,4},{7,5},{8,6},{9,7},{10,... | collective-permute-start | bytes 688136 | tf_op jit(solution)/shard_map/ppermute | solution.py:209
  197.3 10.5 %collective-permute-start.13 = (f32[56,768]{1,0:T(8,128)S(1)}, f32[56,768]{1,0:T(8,128)S(1)}, u32[]{:S(2)}, u32[]{:S(2)}) collective-permute-start(f32[56,768]{1,0:T(8,128)S(1)} %get-tuple-element.56), channel_id=1, source_target_pairs={{0,2},{1,3},{2,4},{3,5},{4,6},{5,7},{6,8},{7,9},{8,10},{9,11},{10,... | collective-permute-start | bytes 516104 | tf_op jit(solution)/shard_map/ppermute | solution.py:208
  200.2 7.6 %collective-permute-start.17 = (f32[56,768]{1,0:T(8,128)S(1)}, f32[56,768]{1,0:T(8,128)S(1)}, u32[]{:S(2)}, u32[]{:S(2)}) collective-permute-start(f32[56,768]{1,0:T(8,128)S(1)} %get-tuple-element.55), channel_id=1, source_target_pairs={{0,14},{1,15},{2,0},{3,1},{4,2},{5,3},{6,4},{7,5},{8,6},{9,7},{10,... | collective-permute-start | bytes 516104 | tf_op jit(solution)/shard_map/ppermute | solution.py:209
  204.9 6.8 %collective-permute-start.4 = (f32[56,1024]{1,0:T(8,128)S(1)}, f32[56,1024]{1,0:T(8,128)S(1)}, u32[]{:S(2)}, u32[]{:S(2)}) collective-permute-start(f32[56,1024]{1,0:T(8,128)S(1)} %get-tuple-element.50), channel_id=1, source_target_pairs={{0,2},{1,3},{2,4},{3,5},{4,6},{5,7},{6,8},{7,9},{8,10},{9,11},{10,... | collective-permute-start | bytes 688136 | tf_op jit(solution)/shard_map/ppermute | solution.py:208
  207.8 7.4 %collective-permute-start.8 = (f32[56,1024]{1,0:T(8,128)S(1)}, f32[56,1024]{1,0:T(8,128)S(1)}, u32[]{:S(2)}, u32[]{:S(2)}) collective-permute-start(f32[56,1024]{1,0:T(8,128)S(1)} %get-tuple-element.49), channel_id=1, source_target_pairs={{0,14},{1,15},{2,0},{3,1},{4,2},{5,3},{6,4},{7,5},{8,6},{9,7},{10,... | collective-permute-start | bytes 688136 | tf_op jit(solution)/shard_map/ppermute | solution.py:209
  207.9 10.6 %collective-permute-start.14 = (f32[56,768]{1,0:T(8,128)S(1)}, f32[56,768]{1,0:T(8,128)S(1)}, u32[]{:S(2)}, u32[]{:S(2)}) collective-permute-start(f32[56,768]{1,0:T(8,128)S(1)} %get-tuple-element.54), channel_id=1, source_target_pairs={{0,2},{1,3},{2,4},{3,5},{4,6},{5,7},{6,8},{7,9},{8,10},{9,11},{10,... | collective-permute-start | bytes 516104 | tf_op jit(solution)/shard_map/ppermute | solution.py:208
  211.4 7.1 %collective-permute-start.18 = (f32[56,768]{1,0:T(8,128)S(1)}, f32[56,768]{1,0:T(8,128)S(1)}, u32[]{:S(2)}, u32[]{:S(2)}) collective-permute-start(f32[56,768]{1,0:T(8,128)S(1)} %get-tuple-element.53), channel_id=1, source_target_pairs={{0,14},{1,15},{2,0},{3,1},{4,2},{5,3},{6,4},{7,5},{8,6},{9,7},{10,... | collective-permute-start | bytes 516104 | tf_op jit(solution)/shard_map/ppermute | solution.py:209
  216.3 6.1 %collective-permute-start.5 = (f32[56,1024]{1,0:T(8,128)S(1)}, f32[56,1024]{1,0:T(8,128)S(1)}, u32[]{:S(2)}, u32[]{:S(2)}) collective-permute-start(f32[56,1024]{1,0:T(8,128)S(1)} %get-tuple-element.48), channel_id=1, source_target_pairs={{0,2},{1,3},{2,4},{3,5},{4,6},{5,7},{6,8},{7,9},{8,10},{9,11},{10,... | collective-permute-start | bytes 688136 | tf_op jit(solution)/shard_map/ppermute | solution.py:208
  218.5 6.0 %collective-permute-start.9 = (f32[56,1024]{1,0:T(8,128)S(1)}, f32[56,1024]{1,0:T(8,128)S(1)}, u32[]{:S(2)}, u32[]{:S(2)}) collective-permute-start(f32[56,1024]{1,0:T(8,128)S(1)} %get-tuple-element.47), channel_id=1, source_target_pairs={{0,14},{1,15},{2,0},{3,1},{4,2},{5,3},{6,4},{7,5},{8,6},{9,7},{10,... | collective-permute-start | bytes 688136 | tf_op jit(solution)/shard_map/ppermute | solution.py:209
  (5 other events, 48.2 us)
Sparse Core Ops, SparseCore 0:
  32.7 125.9 all-gather.1

commit v2 on v1

--- a/solution.py
+++ b/solution.py
@@ -22,7 +22,7 @@
 LIVE = N_DP * BAL
 TILE = 256
 QUARTERS = 4
-WIDTHS = (1024, 768)
+WIDTHS = (768, 1024)
 CLIP = math.sqrt(L * F * D)
 VMEM = 58 * 2**20
 
@@ -121,14 +121,19 @@
     )(place, blocks)
 
 
-def product_kernel(core_ref, factor_ref, turned_ref, *refs):
-    quarters, out_refs, (weighted, total) = refs[:QUARTERS], refs[QUARTERS:-2], refs[-2:]
+def product_kernel(core_ref, factor_ref, *refs):
+    bands, quarters = refs[:QUARTERS], refs[QUARTERS : 2 * QUARTERS]
+    out_refs, (weighted, total) = refs[2 * QUARTERS : -2], refs[-2:]
     for q, ref in enumerate(quarters):
         for k in range(LIVE // QUARTERS):
             e = q * (LIVE // QUARTERS) + k
             rows = ref[k * L : (k + 1) * L, :].astype(jnp.float32)
             weighted[e * L : (e + 1) * L, :] = (factor_ref[e] * rows).astype(jnp.bfloat16)
-    total[...] = jnp.dot(turned_ref[...], weighted[...], preferred_element_type=jnp.float32)
+    height = BLOCK // QUARTERS
+    for q, ref in enumerate(bands):
+        total[q * height : (q + 1) * height, :] = jnp.dot(
+            ref[...], weighted[...], preferred_element_type=jnp.float32
+        )
     core = core_ref[0]
     start = 0
     for c, width in enumerate(WIDTHS):
@@ -162,7 +167,10 @@
     return pl.pallas_call(
         product_kernel,
         grid=(D // TILE,),
-        in_specs=[scalars, scalars, pl.BlockSpec((BLOCK, LIVE * L), lambda i: (0, 0))]
+        in_specs=[scalars, scalars]
+        + [
+            pl.BlockSpec((BLOCK // QUARTERS, LIVE * L), lambda i, q=q: (q, 0)) for q in range(QUARTERS)
+        ]
         + [
             pl.BlockSpec((LIVE * L // QUARTERS, TILE), lambda i, q=q: (q, i)) for q in range(QUARTERS)
         ],
@@ -177,7 +185,7 @@
             flops=2 * LIVE * L * BLOCK * D, bytes_accessed=24 * 2**20, transcendentals=0
         ),
         name="product",
-    )(core, factors, turned, *[cotangents] * QUARTERS)
+    )(core, factors, *[turned] * QUARTERS, *[cotangents] * QUARTERS)
 
 
 def around_z(step):
@@ -220,9 +228,10 @@
     me = lax.axis_index("dp")
     hidden, cotangent = hidden[0, 0], cotangent[0, 0]
     last = lax.dynamic_index_in_dim(cotangent, jnp.clip(counts[0, 0] - 1, 0, POOL - 1), 0, False)
-    last, hidden, counts = lax.optimization_barrier((last, hidden, counts))
+    told = jnp.broadcast_to(counts[:, :, None], (N_DP, 8, L))
+    last, hidden, told = lax.optimization_barrier((last, hidden, told))
     passed = lax.ppermute(last, "dp", [(i, (i + 1) % N_DP) for i in range(N_DP)])
-    held = across_dp(jnp.broadcast_to(counts[:, :, None], (N_DP, 8, L)))[:, 0, 0]
+    held = across_dp(told)[:, 0, 0]
     blocks, factors = prepare(hidden, cotangent, counts)
 
     index = jnp.arange(N_DP, dtype=jnp.int32)
@@ -249,7 +258,11 @@
     core = (lax.axis_index("fsdp") % CORES).astype(jnp.int32).reshape(1)
     core, factors, turned, cotangents = lax.optimization_barrier((core, factors, turned, cotangents))
     chunks = product(core, factors, turned, cotangents)
-    parts = [reduce_begin(keep, other_core(send)) for keep, send in zip(chunks[::2], chunks[1::2])]
+    parts, got = [], core
+    for keep, send in zip(chunks[::2], chunks[1::2]):
+        got, send = lax.optimization_barrier((got, send))
+        got = other_core(send)
+        parts.append(reduce_begin(keep, got))
     for offset in (2, 1, 0):
         sums = []
         for own, up, down in parts:

time: 234 us -> 231 us (0.987)
  transfers between devices with their start and end apart: 22 -> 22, of which waited for: 10 -> 11; matrix products, arithmetic and copies ran while one was open for 5% -> 5% of each run, Pallas kernels for 9% -> 9%
where the time goes in v2:
time: 231 us
  blocking collectives  96.5 us (42%)
  starting transfers between devices  36.2 us (16%)
  waiting for transfers between devices  34.4 us (15%)
  Pallas kernels  32.9 us (14%)
  between operations  14.9 us (6%)
  other arithmetic  12.8 us (6%)
  local copies, waits for them, and re-layouts  2.92 us (1%)
    all_to_all x1, blocking collectives, across_dp(): return lax.all_to_all(value, 'dp', split_axis=0, concat_axis=0, tiled=True)  96.5 us
    ppermute x6, starting transfers between devices, reduce_step(): up = lax.ppermute(up, 'fsdp', around_z(1))  15.5 us
    all_gather x1, waiting for transfers between devices, body(): cotangents = lax.all_gather(chosen, 'dp', axis=0, tiled=True)  13.4 us
    pallas_call x1, Pallas kernels, product(): pl.pallas_call(product_kernel, grid=(D // TILE,), in_specs=[scalars, scal...  13.1 us
    pallas_call x1, Pallas kernels, turn(): pl.pallas_call(turn_kernel, grid_spec=pltpu.PrefetchScalarGridSpec(num_sc...  11.7 us
    all_to_all x2, starting transfers between devices, across_dp(): return lax.all_to_all(value, 'dp', split_axis=0, concat_axis=0, tiled=True)  10.5 us
    pallas_call x1, Pallas kernels, prepare(): pl.pallas_call(prepare_kernel, in_specs=[pl.BlockSpec(memory_space=pltpu....  8.15 us
    ppermute x6, waiting for transfers between devices, reduce_step(): up = lax.ppermute(up, 'fsdp', around_z(1))  7.16 us
  transfers between devices with their start and end apart: 22, of which 11 were waited for; matrix products, arithmetic and copies ran while one was open for 5% of the time, Pallas kernels for 9%

profile of v2, /device:TPU:32, one launch (start us, length us, event | category | flops | bytes accessed | tf_op | source)
XLA Modules:
  0.0 230.6 jit_solution(10442443802151569850)
XLA Ops:
  8.9 7.0 %all-to-all-start = ((s32[16,8,128]{2,1,0:T(8,128)}), s32[16,8,128]{2,1,0:T(8,128)S(1)}, u32[]{:S(2)}, u32[]{:S(2)}) async-start(s32[16,8,128]{2,1,0:T(8,128)} %broadcast_in_dim.48), calls=%async_computation | async-start | bytes 131072 | tf_op jit(solution)/shard_map/all_to_all | solution.py:224
  16.0 2.0 collective-permute-start
  18.0 8.1 %prepare.1 = (bf16[16,2,128,896]{3,2,1,0:T(8,128)(2,1)}, f32[16,8,128]{2,1,0:T(8,128)}) custom-call(s32[1,1]{1,0:T(1,128)} %copy.5.count_ref, bf16[2,128,14336]{2,1,0:T(8,128)(2,1)} %bitcast.44, bf16[2,128,1792]{2,1,0:T(8,128)(2,1)} %bitcast.45), custom_call_target="tpu_custom_call" | custom-call | flops 939524096 | bytes 14680064 | tf_op jit(solution)/shard_map/prepare/pallas_call | solution.py:78
  28.7 3.4 %collective-permute-done = bf16[128,1792]{1,0:T(8,128)(2,1)S(1)} collective-permute-done((bf16[128,1792]{1,0:T(8,128)(2,1)S(1)}, bf16[128,1792]{1,0:T(8,128)(2,1)S(1)}, u32[]{:S(2)}, u32[]{:S(2)}) %collective-permute-start) | collective-permute-done | bytes 458784 | tf_op jit(solution)/shard_map/ppermute | solution.py:233
  32.9 96.5 %all_to_all.15.blocks_ref = bf16[16,256,896]{2,1,0:T(8,128)(2,1)} all-to-all(bf16[16,256,896]{2,1,0:T(8,128)(2,1)} %bitcast.43), channel_id=1, replica_groups=mesh['dp'=16,'fsdp'=16] {'dp'}, dimensions={0} | all-to-all | bytes 14680064 | tf_op jit(solution)/shard_map/all_to_all | solution.py:224
  129.4 3.5 %all-to-all-start.2 = ((f32[16,8,128]{2,1,0:T(8,128)}), f32[16,8,128]{2,1,0:T(8,128)S(1)}, u32[]{:S(2)}, u32[]{:S(2)}) async-start(f32[16,8,128]{2,1,0:T(8,128)} %get-tuple-element.36), calls=%async_computation.2 | async-start | bytes 131072 | tf_op jit(solution)/shard_map/all_to_all | solution.py:224
  133.0 11.7 %turn.1.refs_0_.refs_1_.refs_2_.refs_3_ = bf16[896,2048]{1,0:T(8,128)(2,1)} custom-call(s32[16]{0:T(128)} %get-tuple-element.35.place_ref, bf16[16,256,896]{2,1,0:T(8,128)(2,1)} %all_to_all.15.blocks_ref), custom_call_target="tpu_custom_call" | custom-call | bytes 7340032 | tf_op jit(solution)/shard_map/turn/pallas_call | solution.py:105
  145.5 13.4 %all-gather.2.cloned.1.call-done.refs_4_.refs_5_.refs_6_.refs_7_ = bf16[2048,1792]{1,0:T(8,128)(2,1)} async-done(((bf16[128,1792]{1,0:T(8,128)(2,1)}), bf16[2048,1792]{1,0:T(8,128)(2,1)}) %all-gather.2.cloned.1.call-update) | async-done | bytes 7340048 | tf_op jit(solution)/shard_map/all_gather | solution.py:250
  158.9 13.1 %product.1 = (f32[8,56,768]{2,1,0:T(8,128)}, f32[8,56,768]{2,1,0:T(8,128)}, f32[8,56,1024]{2,1,0:T(8,128)}, f32[8,56,1024]{2,1,0:T(8,128)}) custom-call(s32[1]{0:T(128)} %bitcast.core_ref, f32[16]{0:T(128)} %select_reduce_fusion.factor_ref, bf16[896,2048]{1,0:T(8,128)(2,1)} %turn.1.refs_0_.refs_1_.refs_2_.refs_3_, ...), custom_call_target="tpu_custom_call" | custom-call | flops 6576668672 | bytes 25165824 | tf_op jit(solution)/shard_map/product/pallas_call | solution.py:167
  172.1 3.3 %collective-permute-done.1 = f32[8,56,768]{2,1,0:T(8,128)S(1)} collective-permute-done((f32[8,56,768]{2,1,0:T(8,128)}, f32[8,56,768]{2,1,0:T(8,128)S(1)}, u32[]{:S(2)}, u32[]{:S(2)}) %collective-permute-start.1) | collective-permute-done | bytes 1376288 | tf_op jit(solution)/shard_map/ppermute | solution.py:196
  176.7 1.6 collective-permute-start.2
  181.3 1.6 collective-permute-start.11
  184.3 2.0 bitcast_add_fusion.10
  186.2 1.9 collective-permute-start.3
  188.1 1.4 collective-permute-start.7
  190.8 2.1 collective-permute-start.12
  194.7 2.9 %collective-permute-start.4 = (f32[56,768]{1,0:T(8,128)S(1)}, f32[56,768]{1,0:T(8,128)S(1)}, u32[]{:S(2)}, u32[]{:S(2)}) collective-permute-start(f32[56,768]{1,0:T(8,128)S(1)} %get-tuple-element.60), channel_id=1, source_target_pairs={{0,2},{1,3},{2,4},{3,5},{4,6},{5,7},{6,8},{7,9},{8,10},{9,11},{10,... | collective-permute-start | bytes 516104 | tf_op jit(solution)/shard_map/ppermute | solution.py:216
  197.8 2.8 %collective-permute-done.12 = f32[56,1024]{1,0:T(8,128)S(1)} collective-permute-done((f32[56,1024]{1,0:T(8,128)S(1)}, f32[56,1024]{1,0:T(8,128)S(1)}, u32[]{:S(2)}, u32[]{:S(2)}) %collective-permute-start.12) | collective-permute-done | bytes 229408 | tf_op jit(solution)/shard_map/ppermute | solution.py:216
  202.2 3.0 %collective-permute-start.13 = (f32[56,1024]{1,0:T(8,128)S(1)}, f32[56,1024]{1,0:T(8,128)S(1)}, u32[]{:S(2)}, u32[]{:S(2)}) collective-permute-start(f32[56,1024]{1,0:T(8,128)S(1)} %get-tuple-element.54), channel_id=1, source_target_pairs={{0,2},{1,3},{2,4},{3,5},{4,6},{5,7},{6,8},{7,9},{8,10},{9,11},{10,... | collective-permute-start | bytes 688136 | tf_op jit(solution)/shard_map/ppermute | solution.py:216
  205.3 3.5 %collective-permute-start.5 = (f32[56,768]{1,0:T(8,128)S(1)}, f32[56,768]{1,0:T(8,128)S(1)}, u32[]{:S(2)}, u32[]{:S(2)}) collective-permute-start(f32[56,768]{1,0:T(8,128)S(1)} %get-tuple-element.58), channel_id=1, source_target_pairs={{0,2},{1,3},{2,4},{3,5},{4,6},{5,7},{6,8},{7,9},{8,10},{9,11},{10,... | collective-permute-start | bytes 516104 | tf_op jit(solution)/shard_map/ppermute | solution.py:216
  209.2 3.4 %collective-permute-done.17 = f32[56,1024]{1,0:T(8,128)S(1)} collective-permute-done((f32[56,1024]{1,0:T(8,128)S(1)}, f32[56,1024]{1,0:T(8,128)S(1)}, u32[]{:S(2)}, u32[]{:S(2)}) %collective-permute-start.17) | collective-permute-done | bytes 229408 | tf_op jit(solution)/shard_map/ppermute | solution.py:217
  213.8 2.1 collective-permute-start.14
  215.9 3.9 %collective-permute-done.14 = f32[56,1024]{1,0:T(8,128)S(1)} collective-permute-done((f32[56,1024]{1,0:T(8,128)S(1)}, f32[56,1024]{1,0:T(8,128)S(1)}, u32[]{:S(2)}, u32[]{:S(2)}) %collective-permute-start.14) | collective-permute-done | bytes 229408 | tf_op jit(solution)/shard_map/ppermute | solution.py:216
  219.9 2.0 collective-permute-done.18
  (62 shorter events, 19.4 us)
Async XLA Ops:
  8.9 17.3 %all-to-all-start = ((s32[16,8,128]{2,1,0:T(8,128)}), s32[16,8,128]{2,1,0:T(8,128)S(1)}, u32[]{:S(2)}, u32[]{:S(2)}) async-start(s32[16,8,128]{2,1,0:T(8,128)} %broadcast_in_dim.48), calls=%async_computation | async-start | bytes 131072 | tf_op jit(solution)/shard_map/all_to_all | solution.py:224
  15.9 143.0 %all-gather.2.cloned.1.call-start = ((), (), s32[]{:S(2)}) async-start(), calls=%async_computation.3 | async-start | bytes 7798784 | tf_op jit(solution)/shard_map/all_gather | solution.py:250
  16.0 16.1 %collective-permute-start = (bf16[128,1792]{1,0:T(8,128)(2,1)S(1)}, bf16[128,1792]{1,0:T(8,128)(2,1)S(1)}, u32[]{:S(2)}, u32[]{:S(2)}) collective-permute-start(bf16[128,1792]{1,0:T(8,128)(2,1)S(1)} %dynamic-slice_bitcast_fusion), channel_id=1, source_target_pairs={{0,16},{16,32},{32,48},{48,64},{64,80},{80,96},{96,112},{112,128},... | collective-permute-start | bytes 1376264 | tf_op jit(solution)/shard_map/ppermute | solution.py:233
  129.4 15.2 %all-to-all-start.2 = ((f32[16,8,128]{2,1,0:T(8,128)}), f32[16,8,128]{2,1,0:T(8,128)S(1)}, u32[]{:S(2)}, u32[]{:S(2)}) async-start(f32[16,8,128]{2,1,0:T(8,128)} %get-tuple-element.36), calls=%async_computation.2 | async-start | bytes 131072 | tf_op jit(solution)/shard_map/all_to_all | solution.py:224
  172.0 17.5 %copy-start.1 = (f32[8,56,1024]{2,1,0:T(8,128)S(1)}, f32[8,56,1024]{2,1,0:T(8,128)}, u32[]{:S(2)}) copy-start(f32[8,56,1024]{2,1,0:T(8,128)} %get-tuple-element.46) | copy-start | bytes 5505028
  172.0 3.4 %collective-permute-start.1 = (f32[8,56,768]{2,1,0:T(8,128)}, f32[8,56,768]{2,1,0:T(8,128)S(1)}, u32[]{:S(2)}, u32[]{:S(2)}) collective-permute-start(f32[8,56,768]{2,1,0:T(8,128)} %get-tuple-element.45), channel_id=1, source_target_pairs={{0,1},{1,0},{2,3},{3,2},{4,5},{5,4},{6,7},{7,6},{8,9},{9,8},{10,11... | collective-permute-start | bytes 4128776 | tf_op jit(solution)/shard_map/ppermute | solution.py:196
  175.4 4.1 %collective-permute-start.10 = (f32[8,56,1024]{2,1,0:T(8,128)}, f32[8,56,1024]{2,1,0:T(8,128)}, u32[]{:S(2)}, u32[]{:S(2)}) collective-permute-start(f32[8,56,1024]{2,1,0:T(8,128)} %get-tuple-element.48), channel_id=1, source_target_pairs={{0,1},{1,0},{2,3},{3,2},{4,5},{5,4},{6,7},{7,6},{8,9},{9,8},{10,11... | collective-permute-start | bytes 5505032 | tf_op jit(solution)/shard_map/ppermute | solution.py:196
  176.7 7.5 %collective-permute-start.2 = (f32[56,384]{1,0:T(8,128)S(1)}, f32[56,384]{1,0:T(8,128)S(1)}, u32[]{:S(2)}, u32[]{:S(2)}) collective-permute-start(f32[56,384]{1,0:T(8,128)S(1)} %get-tuple-element.66), channel_id=1, source_target_pairs={{0,2},{1,3},{2,4},{3,5},{4,6},{5,7},{6,8},{7,9},{8,10},{9,11},{10,... | collective-permute-start | bytes 258056 | tf_op jit(solution)/shard_map/ppermute | solution.py:208
  178.4 5.9 %collective-permute-start.6 = (f32[56,384]{1,0:T(8,128)S(1)}, f32[56,384]{1,0:T(8,128)S(1)}, u32[]{:S(2)}, u32[]{:S(2)}) collective-permute-start(f32[56,384]{1,0:T(8,128)S(1)} %get-tuple-element.65), channel_id=1, source_target_pairs={{0,14},{1,15},{2,0},{3,1},{4,2},{5,3},{6,4},{7,5},{8,6},{9,7},{10,... | collective-permute-start | bytes 258056 | tf_op jit(solution)/shard_map/ppermute | solution.py:209
  181.3 8.1 %collective-permute-start.11 = (f32[56,512]{1,0:T(8,128)}, f32[56,512]{1,0:T(8,128)}, u32[]{:S(2)}, u32[]{:S(2)}) collective-permute-start(f32[56,512]{1,0:T(8,128)} %get-tuple-element.64), channel_id=1, source_target_pairs={{0,2},{1,3},{2,4},{3,5},{4,6},{5,7},{6,8},{7,9},{8,10},{9,11},{10,... | collective-permute-start | bytes 344072 | tf_op jit(solution)/shard_map/ppermute | solution.py:208
  182.9 6.5 %collective-permute-start.15 = (f32[56,512]{1,0:T(8,128)}, f32[56,512]{1,0:T(8,128)}, u32[]{:S(2)}, u32[]{:S(2)}) collective-permute-start(f32[56,512]{1,0:T(8,128)} %get-tuple-element.63), channel_id=1, source_target_pairs={{0,14},{1,15},{2,0},{3,1},{4,2},{5,3},{6,4},{7,5},{8,6},{9,7},{10,... | collective-permute-start | bytes 344072 | tf_op jit(solution)/shard_map/ppermute | solution.py:209
  186.2 8.0 %collective-permute-start.3 = (f32[56,768]{1,0:T(8,128)}, f32[56,768]{1,0:T(8,128)S(1)}, u32[]{:S(2)}, u32[]{:S(2)}) collective-permute-start(f32[56,768]{1,0:T(8,128)} %get-tuple-element.62), channel_id=1, source_target_pairs={{0,2},{1,3},{2,4},{3,5},{4,6},{5,7},{6,8},{7,9},{8,10},{9,11},{10,... | collective-permute-start | bytes 516104 | tf_op jit(solution)/shard_map/ppermute | solution.py:216
  188.1 6.6 %collective-permute-start.7 = (f32[56,768]{1,0:T(8,128)}, f32[56,768]{1,0:T(8,128)S(1)}, u32[]{:S(2)}, u32[]{:S(2)}) collective-permute-start(f32[56,768]{1,0:T(8,128)} %get-tuple-element.61), channel_id=1, source_target_pairs={{0,14},{1,15},{2,0},{3,1},{4,2},{5,3},{6,4},{7,5},{8,6},{9,7},{10,... | collective-permute-start | bytes 516104 | tf_op jit(solution)/shard_map/ppermute | solution.py:217
  190.8 9.8 %collective-permute-start.12 = (f32[56,1024]{1,0:T(8,128)S(1)}, f32[56,1024]{1,0:T(8,128)S(1)}, u32[]{:S(2)}, u32[]{:S(2)}) collective-permute-start(f32[56,1024]{1,0:T(8,128)S(1)} %get-tuple-element.56), channel_id=1, source_target_pairs={{0,2},{1,3},{2,4},{3,5},{4,6},{5,7},{6,8},{7,9},{8,10},{9,11},{10,... | collective-permute-start | bytes 688136 | tf_op jit(solution)/shard_map/ppermute | solution.py:216
  192.9 8.2 %collective-permute-start.16 = (f32[56,1024]{1,0:T(8,128)S(1)}, f32[56,1024]{1,0:T(8,128)S(1)}, u32[]{:S(2)}, u32[]{:S(2)}) collective-permute-start(f32[56,1024]{1,0:T(8,128)S(1)} %get-tuple-element.55), channel_id=1, source_target_pairs={{0,14},{1,15},{2,0},{3,1},{4,2},{5,3},{6,4},{7,5},{8,6},{9,7},{10,... | collective-permute-start | bytes 688136 | tf_op jit(solution)/shard_map/ppermute | solution.py:217
  194.7 10.5 %collective-permute-start.4 = (f32[56,768]{1,0:T(8,128)S(1)}, f32[56,768]{1,0:T(8,128)S(1)}, u32[]{:S(2)}, u32[]{:S(2)}) collective-permute-start(f32[56,768]{1,0:T(8,128)S(1)} %get-tuple-element.60), channel_id=1, source_target_pairs={{0,2},{1,3},{2,4},{3,5},{4,6},{5,7},{6,8},{7,9},{8,10},{9,11},{10,... | collective-permute-start | bytes 516104 | tf_op jit(solution)/shard_map/ppermute | solution.py:216
  197.6 7.6 %collective-permute-start.8 = (f32[56,768]{1,0:T(8,128)S(1)}, f32[56,768]{1,0:T(8,128)S(1)}, u32[]{:S(2)}, u32[]{:S(2)}) collective-permute-start(f32[56,768]{1,0:T(8,128)S(1)} %get-tuple-element.59), channel_id=1, source_target_pairs={{0,14},{1,15},{2,0},{3,1},{4,2},{5,3},{6,4},{7,5},{8,6},{9,7},{10,... | collective-permute-start | bytes 516104 | tf_op jit(solution)/shard_map/ppermute | solution.py:217
  202.2 7.0 %collective-permute-start.13 = (f32[56,1024]{1,0:T(8,128)S(1)}, f32[56,1024]{1,0:T(8,128)S(1)}, u32[]{:S(2)}, u32[]{:S(2)}) collective-permute-start(f32[56,1024]{1,0:T(8,128)S(1)} %get-tuple-element.54), channel_id=1, source_target_pairs={{0,2},{1,3},{2,4},{3,5},{4,6},{5,7},{6,8},{7,9},{8,10},{9,11},{10,... | collective-permute-start | bytes 688136 | tf_op jit(solution)/shard_map/ppermute | solution.py:216
  205.2 7.4 %collective-permute-start.17 = (f32[56,1024]{1,0:T(8,128)S(1)}, f32[56,1024]{1,0:T(8,128)S(1)}, u32[]{:S(2)}, u32[]{:S(2)}) collective-permute-start(f32[56,1024]{1,0:T(8,128)S(1)} %get-tuple-element.53), channel_id=1, source_target_pairs={{0,14},{1,15},{2,0},{3,1},{4,2},{5,3},{6,4},{7,5},{8,6},{9,7},{10,... | collective-permute-start | bytes 688136 | tf_op jit(solution)/shard_map/ppermute | solution.py:217
  205.3 10.6 %collective-permute-start.5 = (f32[56,768]{1,0:T(8,128)S(1)}, f32[56,768]{1,0:T(8,128)S(1)}, u32[]{:S(2)}, u32[]{:S(2)}) collective-permute-start(f32[56,768]{1,0:T(8,128)S(1)} %get-tuple-element.58), channel_id=1, source_target_pairs={{0,2},{1,3},{2,4},{3,5},{4,6},{5,7},{6,8},{7,9},{8,10},{9,11},{10,... | collective-permute-start | bytes 516104 | tf_op jit(solution)/shard_map/ppermute | solution.py:216
  208.8 14.1 %copy-start.5 = (f32[56,1792]{1,0:T(8,128)S(1)}, f32[56,1792]{1,0:T(8,128)}, u32[]{:S(2)}) copy-start(f32[56,1792]{1,0:T(8,128)} %param.7) | copy-start | bytes 1204228
  208.8 7.1 %collective-permute-start.9 = (f32[56,768]{1,0:T(8,128)S(1)}, f32[56,768]{1,0:T(8,128)S(1)}, u32[]{:S(2)}, u32[]{:S(2)}) collective-permute-start(f32[56,768]{1,0:T(8,128)S(1)} %get-tuple-element.57), channel_id=1, source_target_pairs={{0,14},{1,15},{2,0},{3,1},{4,2},{5,3},{6,4},{7,5},{8,6},{9,7},{10,... | collective-permute-start | bytes 516104 | tf_op jit(solution)/shard_map/ppermute | solution.py:217
  213.8 6.1 %collective-permute-start.14 = (f32[56,1024]{1,0:T(8,128)S(1)}, f32[56,1024]{1,0:T(8,128)S(1)}, u32[]{:S(2)}, u32[]{:S(2)}) collective-permute-start(f32[56,1024]{1,0:T(8,128)S(1)} %get-tuple-element.52), channel_id=1, source_target_pairs={{0,2},{1,3},{2,4},{3,5},{4,6},{5,7},{6,8},{7,9},{8,10},{9,11},{10,... | collective-permute-start | bytes 688136 | tf_op jit(solution)/shard_map/ppermute | solution.py:216
  215.9 6.0 %collective-permute-start.18 = (f32[56,1024]{1,0:T(8,128)S(1)}, f32[56,1024]{1,0:T(8,128)S(1)}, u32[]{:S(2)}, u32[]{:S(2)}) collective-permute-start(f32[56,1024]{1,0:T(8,128)S(1)} %get-tuple-element.51), channel_id=1, source_target_pairs={{0,14},{1,15},{2,0},{3,1},{4,2},{5,3},{6,4},{7,5},{8,6},{9,7},{10,... | collective-permute-start | bytes 688136 | tf_op jit(solution)/shard_map/ppermute | solution.py:217
  (5 other events, 49.4 us)
Sparse Core Ops, SparseCore 0:
  33.0 125.8 all-gather.1

commit v3 on v1

--- a/solution.py
+++ b/solution.py
@@ -22,9 +22,9 @@
 LIVE = N_DP * BAL
 TILE = 256
 QUARTERS = 4
-WIDTHS = (1024, 768)
+WIDTHS = (768, 1024)
 CLIP = math.sqrt(L * F * D)
-VMEM = 58 * 2**20
+VMEM = 48 * 2**20
 
 
 def prepare_kernel(count_ref, hidden_ref, cotangent_ref, blocks_ref, factor_ref, rows_buf, other_buf, gram, sems):
@@ -89,7 +89,7 @@
             pltpu.VMEM((TOK, TOK), jnp.float32),
             pltpu.SemaphoreType.DMA((3, N_DP)),
         ],
-        compiler_params=pltpu.CompilerParams(vmem_limit_bytes=VMEM),
+        compiler_params=pltpu.CompilerParams(vmem_limit_bytes=VMEM + 12 * 2**20),
         cost_estimate=pl.CostEstimate(
             flops=2 * TOK * L * F, bytes_accessed=4 * TOK * F, transcendentals=0
         ),
@@ -122,7 +122,7 @@
 
 
 def product_kernel(core_ref, factor_ref, turned_ref, *refs):
-    quarters, out_refs, (weighted, total) = refs[:QUARTERS], refs[QUARTERS:-2], refs[-2:]
+    quarters, (keep_ref, send_ref, weighted, total) = refs[:QUARTERS], refs[QUARTERS:]
     for q, ref in enumerate(quarters):
         for k in range(LIVE // QUARTERS):
             e = q * (LIVE // QUARTERS) + k
@@ -130,51 +130,34 @@
             weighted[e * L : (e + 1) * L, :] = (factor_ref[e] * rows).astype(jnp.bfloat16)
     total[...] = jnp.dot(turned_ref[...], weighted[...], preferred_element_type=jnp.float32)
     core = core_ref[0]
-    start = 0
-    for c, width in enumerate(WIDTHS):
-        end = start + width // TILE
-
-        @pl.when((pl.program_id(0) >= start) & (pl.program_id(0) < end))
-        def _(keep_ref=out_refs[2 * c], send_ref=out_refs[2 * c + 1]):
-            for z in range(NZ):
-                base = z * CORES * ROWS
-                mine = pl.multiple_of(base + core * ROWS, 8)
-                others = pl.multiple_of(base + (1 - core) * ROWS, 8)
-                keep_ref[z] = total[pl.ds(mine, ROWS), :]
-                send_ref[z] = total[pl.ds(others, ROWS), :]
-
-        start = end
-
-
-def product(core, factors, turned, cotangents):
+    for z in range(NZ):
+        base = z * CORES * ROWS
+        mine = pl.multiple_of(base + core * ROWS, 8)
+        others = pl.multiple_of(base + (1 - core) * ROWS, 8)
+        keep_ref[z] = total[pl.ds(mine, ROWS), :]
+        send_ref[z] = total[pl.ds(others, ROWS), :]
+
+
+def product(core, factors, turned, cotangents, start, width):
+    out = jax.ShapeDtypeStruct((NZ, ROWS, width), jnp.float32)
     scalars = pl.BlockSpec(memory_space=pltpu.SMEM)
-    out_specs, out_shape = [], []
-    start = 0
-    for width in WIDTHS:
-        tiles = width // TILE
-
-        def at(i, start=start, tiles=tiles):
-            return (0, 0, jnp.clip(i - start, 0, tiles - 1))
-
-        out_specs += [pl.BlockSpec((NZ, ROWS, TILE), at)] * 2
-        out_shape += [jax.ShapeDtypeStruct((NZ, ROWS, width), jnp.float32)] * 2
-        start += tiles
     return pl.pallas_call(
         product_kernel,
-        grid=(D // TILE,),
+        grid=(width // TILE,),
         in_specs=[scalars, scalars, pl.BlockSpec((BLOCK, LIVE * L), lambda i: (0, 0))]
         + [
-            pl.BlockSpec((LIVE * L // QUARTERS, TILE), lambda i, q=q: (q, i)) for q in range(QUARTERS)
-        ],
-        out_specs=out_specs,
-        out_shape=out_shape,
+            pl.BlockSpec((LIVE * L // QUARTERS, TILE), lambda i, q=q: (q, start // TILE + i))
+            for q in range(QUARTERS)
+        ],
+        out_specs=[pl.BlockSpec((NZ, ROWS, TILE), lambda i: (0, 0, i))] * 2,
+        out_shape=[out, out],
         scratch_shapes=[
             pltpu.VMEM((LIVE * L, TILE), jnp.bfloat16),
             pltpu.VMEM((BLOCK, TILE), jnp.float32),
         ],
-        compiler_params=pltpu.CompilerParams(vmem_limit_bytes=VMEM),
+        compiler_params=pltpu.CompilerParams(vmem_limit_bytes=58 * 2**20),
         cost_estimate=pl.CostEstimate(
-            flops=2 * LIVE * L * BLOCK * D, bytes_accessed=24 * 2**20, transcendentals=0
+            flops=2 * LIVE * L * BLOCK * width, bytes_accessed=12 * 2**20, transcendentals=0
         ),
         name="product",
     )(core, factors, turned, *[cotangents] * QUARTERS)
@@ -248,8 +231,12 @@
     turned = turn(place, blocks)
     core = (lax.axis_index("fsdp") % CORES).astype(jnp.int32).reshape(1)
     core, factors, turned, cotangents = lax.optimization_barrier((core, factors, turned, cotangents))
-    chunks = product(core, factors, turned, cotangents)
-    parts = [reduce_begin(keep, other_core(send)) for keep, send in zip(chunks[::2], chunks[1::2])]
+    parts, got = [], core
+    for i, width in enumerate(WIDTHS):
+        keep, send = product(core, factors, turned, cotangents, sum(WIDTHS[:i]), width)
+        got, send = lax.optimization_barrier((got, send))
+        got = other_core(send)
+        parts.append(reduce_begin(keep, got))
     for offset in (2, 1, 0):
         sums = []
         for own, up, down in parts:

time: 234 us -> 231 us (0.987)
  waiting for transfers between devices: 35.7 us -> 30.3 us
    ppermute x2, waiting for transfers between devices: 5.46 us -> 0.64 us  [other_core(): return lax.ppermute(send, 'fsdp', [(i, i ^ 1) for i in range(N_FSDP)])]
    pallas_call x1 -> x2, Pallas kernels: 13.3 us -> 16.1 us  [product(): pl.pallas_call(product_kernel, grid=(width // TILE,), in_specs=[scalars,...]
    ppermute x6, waiting for transfers between devices: 6.92 us -> 4.52 us  [reduce_step(): up = lax.ppermute(up, 'fsdp', around_z(1))]
  transfers between devices with their start and end apart: 22 -> 22, of which waited for: 10 -> 12; matrix products, arithmetic and copies ran while one was open for 5% -> 6% of each run, Pallas kernels for 9% -> 12%
where the time goes in v3:
time: 231 us; the launch traced here: 230 us
  blocking collectives  96.6 us (42%)
  starting transfers between devices  35 us (15%)
  Pallas kernels  34.2 us (15%)
  waiting for transfers between devices  30.3 us (13%)
  between operations  14.8 us (6%)
  other arithmetic  14.6 us (6%)
  local copies, waits for them, and re-layouts  4.85 us (2%)
    all_to_all x1, blocking collectives, across_dp(): return lax.all_to_all(value, 'dp', split_axis=0, concat_axis=0, tiled=True)  96.6 us
    pallas_call x2, Pallas kernels, product(): pl.pallas_call(product_kernel, grid=(width // TILE,), in_specs=[scalars,...  16.1 us
    ppermute x6, starting transfers between devices, reduce_step(): up = lax.ppermute(up, 'fsdp', around_z(1))  13.8 us
    all_gather x1, waiting for transfers between devices, body(): cotangents = lax.all_gather(chosen, 'dp', axis=0, tiled=True)  13.2 us
    all_to_all x2, starting transfers between devices, across_dp(): return lax.all_to_all(value, 'dp', split_axis=0, concat_axis=0, tiled=True)  10.5 us
    pallas_call x1, Pallas kernels, turn(): pl.pallas_call(turn_kernel, grid_spec=pltpu.PrefetchScalarGridSpec(num_sc...  10 us
    pallas_call x1, Pallas kernels, prepare(): pl.pallas_call(prepare_kernel, in_specs=[pl.BlockSpec(memory_space=pltpu....  8.15 us
    ppermute x6, waiting for transfers between devices, reduce_step(): down = lax.ppermute(down, 'fsdp', around_z(-1))  8.07 us
  transfers between devices with their start and end apart: 22, of which 12 were waited for; matrix products, arithmetic and copies ran while one was open for 6% of the time, Pallas kernels for 12%

profile of v3, /device:TPU:32, one launch (start us, length us, event | category | flops | bytes accessed | tf_op | source)
XLA Modules:
  0.0 230.4 jit_solution(15757658501048740797)
XLA Ops:
  7.8 7.0 %all-to-all-start = ((s32[16,8,128]{2,1,0:T(8,128)}), s32[16,8,128]{2,1,0:T(8,128)S(1)}, u32[]{:S(2)}, u32[]{:S(2)}) async-start(s32[16,8,128]{2,1,0:T(8,128)} %broadcast_in_dim.51), calls=%async_computation | async-start | bytes 131072 | tf_op jit(solution)/shard_map/all_to_all | solution.py:199
  16.0 2.0 collective-permute-start
  18.0 8.1 %prepare.1 = (bf16[16,2,128,896]{3,2,1,0:T(8,128)(2,1)}, f32[16,8,128]{2,1,0:T(8,128)}) custom-call(s32[1,1]{1,0:T(1,128)} %copy.5.count_ref, bf16[2,128,14336]{2,1,0:T(8,128)(2,1)} %bitcast.44, bf16[2,128,1792]{2,1,0:T(8,128)(2,1)} %bitcast.45), custom_call_target="tpu_custom_call" | custom-call | flops 939524096 | bytes 14680064 | tf_op jit(solution)/shard_map/prepare/pallas_call | solution.py:78
  27.9 3.8 %collective-permute-done = bf16[128,1792]{1,0:T(8,128)(2,1)S(1)} collective-permute-done((bf16[128,1792]{1,0:T(8,128)(2,1)S(1)}, bf16[128,1792]{1,0:T(8,128)(2,1)S(1)}, u32[]{:S(2)}, u32[]{:S(2)}) %collective-permute-start) | collective-permute-done | bytes 458784 | tf_op jit(solution)/shard_map/ppermute | solution.py:207
  32.6 96.6 %all_to_all.15.blocks_ref = bf16[16,256,896]{2,1,0:T(8,128)(2,1)} all-to-all(bf16[16,256,896]{2,1,0:T(8,128)(2,1)} %bitcast.43), channel_id=1, replica_groups=mesh['dp'=16,'fsdp'=16] {'dp'}, dimensions={0} | all-to-all | bytes 14680064 | tf_op jit(solution)/shard_map/all_to_all | solution.py:199
  129.2 3.5 %all-to-all-start.2 = ((f32[16,8,128]{2,1,0:T(8,128)}), f32[16,8,128]{2,1,0:T(8,128)S(1)}, u32[]{:S(2)}, u32[]{:S(2)}) async-start(f32[16,8,128]{2,1,0:T(8,128)} %get-tuple-element.36), calls=%async_computation.2 | async-start | bytes 131072 | tf_op jit(solution)/shard_map/all_to_all | solution.py:199
  132.8 10.0 %turn.1.turned_ref = bf16[896,2048]{1,0:T(8,128)(2,1)S(1)} custom-call(s32[16]{0:T(128)S(1)} %get-tuple-element.35.place_ref, bf16[16,256,896]{2,1,0:T(8,128)(2,1)} %all_to_all.15.blocks_ref), custom_call_target="tpu_custom_call" | custom-call | bytes 7340032 | tf_op jit(solution)/shard_map/turn/pallas_call | solution.py:105
  142.8 1.9 copy-done
  145.5 13.2 %all-gather.2.cloned.1.call-done.refs_0_.refs_1_.refs_2_.refs_3_ = bf16[2048,1792]{1,0:T(8,128)(2,1)} async-done(((bf16[128,1792]{1,0:T(8,128)(2,1)}), bf16[2048,1792]{1,0:T(8,128)(2,1)}) %all-gather.2.cloned.1.call-update) | async-done | bytes 7340048 | tf_op jit(solution)/shard_map/all_gather | solution.py:224
  158.8 7.3 %product.2 = (f32[8,56,768]{2,1,0:T(8,128)}, f32[8,56,768]{2,1,0:T(8,128)}) custom-call(s32[1]{0:T(128)} %bitcast.core_ref, f32[16]{0:T(128)} %select_reduce_fusion.factor_ref, bf16[896,2048]{1,0:T(8,128)(2,1)} %copy-done, bf16[2048,1792]{1,0:T(8,128)(2,1)} %all-gather.2.cloned.1.call-done.refs_0_.refs_1_.refs_2_.refs_3_, ...), custom_call_target="tpu_custom_call" | custom-call | flops 2818572288 | bytes 12582912 | tf_op jit(solution)/shard_map/product/pallas_call | solution.py:144
  166.2 8.7 %product.3 = (f32[8,56,1024]{2,1,0:T(8,128)}, f32[8,56,1024]{2,1,0:T(8,128)}) custom-call(s32[1]{0:T(128)} %bitcast.core_ref, f32[16]{0:T(128)} %select_reduce_fusion.factor_ref, bf16[896,2048]{1,0:T(8,128)(2,1)} %copy-done, bf16[2048,1792]{1,0:T(8,128)(2,1)} %all-gather.2.cloned.1.call-done.refs_0_.refs_1_.refs_2_.refs_3_, ...), custom_call_target="tpu_custom_call" | custom-call | flops 3758096384 | bytes 12582912 | tf_op jit(solution)/shard_map/product/pallas_call | solution.py:144
  176.4 1.7 collective-permute-start.2
  181.0 1.6 collective-permute-start.11
  184.0 1.8 bitcast_add_fusion.10
  185.7 1.8 collective-permute-start.3
  187.6 1.4 collective-permute-start.7
  190.3 2.4 %collective-permute-start.12 = (f32[56,1024]{1,0:T(8,128)S(1)}, f32[56,1024]{1,0:T(8,128)S(1)}, u32[]{:S(2)}, u32[]{:S(2)}) collective-permute-start(f32[56,1024]{1,0:T(8,128)S(1)} %get-tuple-element.56), channel_id=1, source_target_pairs={{0,2},{1,3},{2,4},{3,5},{4,6},{5,7},{6,8},{7,9},{8,10},{9,11},{10,... | collective-permute-start | bytes 688136 | tf_op jit(solution)/shard_map/ppermute | solution.py:191
  195.3 2.7 %collective-permute-start.4 = (f32[56,768]{1,0:T(8,128)S(1)}, f32[56,768]{1,0:T(8,128)S(1)}, u32[]{:S(2)}, u32[]{:S(2)}) collective-permute-start(f32[56,768]{1,0:T(8,128)S(1)} %get-tuple-element.60), channel_id=1, source_target_pairs={{0,2},{1,3},{2,4},{3,5},{4,6},{5,7},{6,8},{7,9},{8,10},{9,11},{10,... | collective-permute-start | bytes 516104 | tf_op jit(solution)/shard_map/ppermute | solution.py:191
  201.2 2.6 %collective-permute-start.13 = (f32[56,1024]{1,0:T(8,128)S(1)}, f32[56,1024]{1,0:T(8,128)S(1)}, u32[]{:S(2)}, u32[]{:S(2)}) collective-permute-start(f32[56,1024]{1,0:T(8,128)S(1)} %get-tuple-element.54), channel_id=1, source_target_pairs={{0,2},{1,3},{2,4},{3,5},{4,6},{5,7},{6,8},{7,9},{8,10},{9,11},{10,... | collective-permute-start | bytes 688136 | tf_op jit(solution)/shard_map/ppermute | solution.py:191
  206.1 2.5 %collective-permute-start.5 = (f32[56,768]{1,0:T(8,128)S(1)}, f32[56,768]{1,0:T(8,128)S(1)}, u32[]{:S(2)}, u32[]{:S(2)}) collective-permute-start(f32[56,768]{1,0:T(8,128)S(1)} %get-tuple-element.58), channel_id=1, source_target_pairs={{0,2},{1,3},{2,4},{3,5},{4,6},{5,7},{6,8},{7,9},{8,10},{9,11},{10,... | collective-permute-start | bytes 516104 | tf_op jit(solution)/shard_map/ppermute | solution.py:191
  209.2 3.5 %collective-permute-done.17 = f32[56,1024]{1,0:T(8,128)S(1)} collective-permute-done((f32[56,1024]{1,0:T(8,128)S(1)}, f32[56,1024]{1,0:T(8,128)S(1)}, u32[]{:S(2)}, u32[]{:S(2)}) %collective-permute-start.17) | collective-permute-done | bytes 229408 | tf_op jit(solution)/shard_map/ppermute | solution.py:192
  213.9 1.8 collective-permute-start.14
  217.2 2.8 %collective-permute-done.14 = f32[56,1024]{1,0:T(8,128)S(1)} collective-permute-done((f32[56,1024]{1,0:T(8,128)S(1)}, f32[56,1024]{1,0:T(8,128)S(1)}, u32[]{:S(2)}, u32[]{:S(2)}) %collective-permute-start.14) | collective-permute-done | bytes 229408 | tf_op jit(solution)/shard_map/ppermute | solution.py:191
  220.0 1.7 collective-permute-done.18
  (59 shorter events, 24.8 us)
Async XLA Ops:
  7.8 18.3 %all-to-all-start = ((s32[16,8,128]{2,1,0:T(8,128)}), s32[16,8,128]{2,1,0:T(8,128)S(1)}, u32[]{:S(2)}, u32[]{:S(2)}) async-start(s32[16,8,128]{2,1,0:T(8,128)} %broadcast_in_dim.51), calls=%async_computation | async-start | bytes 131072 | tf_op jit(solution)/shard_map/all_to_all | solution.py:199
  14.9 143.9 %all-gather.2.cloned.1.call-start = ((), (), s32[]{:S(2)}) async-start(), calls=%async_computation.3 | async-start | bytes 7798784 | tf_op jit(solution)/shard_map/all_gather | solution.py:224
  16.0 15.8 %collective-permute-start = (bf16[128,1792]{1,0:T(8,128)(2,1)S(1)}, bf16[128,1792]{1,0:T(8,128)(2,1)S(1)}, u32[]{:S(2)}, u32[]{:S(2)}) collective-permute-start(bf16[128,1792]{1,0:T(8,128)(2,1)S(1)} %dynamic-slice_bitcast_fusion), channel_id=1, source_target_pairs={{0,16},{16,32},{32,48},{48,64},{64,80},{80,96},{96,112},{112,128},... | collective-permute-start | bytes 1376264 | tf_op jit(solution)/shard_map/ppermute | solution.py:207
  129.2 15.5 %all-to-all-start.2 = ((f32[16,8,128]{2,1,0:T(8,128)}), f32[16,8,128]{2,1,0:T(8,128)S(1)}, u32[]{:S(2)}, u32[]{:S(2)}) async-start(f32[16,8,128]{2,1,0:T(8,128)} %get-tuple-element.36), calls=%async_computation.2 | async-start | bytes 131072 | tf_op jit(solution)/shard_map/all_to_all | solution.py:199
  166.1 8.8 %collective-permute-start.1 = (f32[8,56,768]{2,1,0:T(8,128)}, f32[8,56,768]{2,1,0:T(8,128)}, u32[]{:S(2)}, u32[]{:S(2)}) collective-permute-start(f32[8,56,768]{2,1,0:T(8,128)} %get-tuple-element.45), channel_id=1, source_target_pairs={{0,1},{1,0},{2,3},{3,2},{4,5},{5,4},{6,7},{7,6},{8,9},{9,8},{10,11... | collective-permute-start | bytes 4128776 | tf_op jit(solution)/shard_map/ppermute | solution.py:171
  174.9 14.1 %copy-start.2 = (f32[8,56,1024]{2,1,0:T(8,128)S(1)}, f32[8,56,1024]{2,1,0:T(8,128)}, u32[]{:S(2)}) copy-start(f32[8,56,1024]{2,1,0:T(8,128)} %get-tuple-element.46) | copy-start | bytes 5505028
  174.9 4.3 %collective-permute-start.10 = (f32[8,56,1024]{2,1,0:T(8,128)}, f32[8,56,1024]{2,1,0:T(8,128)}, u32[]{:S(2)}, u32[]{:S(2)}) collective-permute-start(f32[8,56,1024]{2,1,0:T(8,128)} %get-tuple-element.48), channel_id=1, source_target_pairs={{0,1},{1,0},{2,3},{3,2},{4,5},{5,4},{6,7},{7,6},{8,9},{9,8},{10,11... | collective-permute-start | bytes 5505032 | tf_op jit(solution)/shard_map/ppermute | solution.py:171
  176.4 7.5 %collective-permute-start.2 = (f32[56,384]{1,0:T(8,128)S(1)}, f32[56,384]{1,0:T(8,128)S(1)}, u32[]{:S(2)}, u32[]{:S(2)}) collective-permute-start(f32[56,384]{1,0:T(8,128)S(1)} %get-tuple-element.66), channel_id=1, source_target_pairs={{0,2},{1,3},{2,4},{3,5},{4,6},{5,7},{6,8},{7,9},{8,10},{9,11},{10,... | collective-permute-start | bytes 258056 | tf_op jit(solution)/shard_map/ppermute | solution.py:183
  178.1 5.8 %collective-permute-start.6 = (f32[56,384]{1,0:T(8,128)S(1)}, f32[56,384]{1,0:T(8,128)S(1)}, u32[]{:S(2)}, u32[]{:S(2)}) collective-permute-start(f32[56,384]{1,0:T(8,128)S(1)} %get-tuple-element.65), channel_id=1, source_target_pairs={{0,14},{1,15},{2,0},{3,1},{4,2},{5,3},{6,4},{7,5},{8,6},{9,7},{10,... | collective-permute-start | bytes 258056 | tf_op jit(solution)/shard_map/ppermute | solution.py:184
  181.0 8.0 %collective-permute-start.11 = (f32[56,512]{1,0:T(8,128)}, f32[56,512]{1,0:T(8,128)}, u32[]{:S(2)}, u32[]{:S(2)}) collective-permute-start(f32[56,512]{1,0:T(8,128)} %get-tuple-element.64), channel_id=1, source_target_pairs={{0,2},{1,3},{2,4},{3,5},{4,6},{5,7},{6,8},{7,9},{8,10},{9,11},{10,... | collective-permute-start | bytes 344072 | tf_op jit(solution)/shard_map/ppermute | solution.py:183
  182.6 6.4 %collective-permute-start.15 = (f32[56,512]{1,0:T(8,128)}, f32[56,512]{1,0:T(8,128)}, u32[]{:S(2)}, u32[]{:S(2)}) collective-permute-start(f32[56,512]{1,0:T(8,128)} %get-tuple-element.63), channel_id=1, source_target_pairs={{0,14},{1,15},{2,0},{3,1},{4,2},{5,3},{6,4},{7,5},{8,6},{9,7},{10,... | collective-permute-start | bytes 344072 | tf_op jit(solution)/shard_map/ppermute | solution.py:184
  185.7 8.1 %collective-permute-start.3 = (f32[56,768]{1,0:T(8,128)}, f32[56,768]{1,0:T(8,128)S(1)}, u32[]{:S(2)}, u32[]{:S(2)}) collective-permute-start(f32[56,768]{1,0:T(8,128)} %get-tuple-element.62), channel_id=1, source_target_pairs={{0,2},{1,3},{2,4},{3,5},{4,6},{5,7},{6,8},{7,9},{8,10},{9,11},{10,... | collective-permute-start | bytes 516104 | tf_op jit(solution)/shard_map/ppermute | solution.py:191
  187.6 6.7 %collective-permute-start.7 = (f32[56,768]{1,0:T(8,128)}, f32[56,768]{1,0:T(8,128)S(1)}, u32[]{:S(2)}, u32[]{:S(2)}) collective-permute-start(f32[56,768]{1,0:T(8,128)} %get-tuple-element.61), channel_id=1, source_target_pairs={{0,14},{1,15},{2,0},{3,1},{4,2},{5,3},{6,4},{7,5},{8,6},{9,7},{10,... | collective-permute-start | bytes 516104 | tf_op jit(solution)/shard_map/ppermute | solution.py:192
  190.3 9.0 %collective-permute-start.12 = (f32[56,1024]{1,0:T(8,128)S(1)}, f32[56,1024]{1,0:T(8,128)S(1)}, u32[]{:S(2)}, u32[]{:S(2)}) collective-permute-start(f32[56,1024]{1,0:T(8,128)S(1)} %get-tuple-element.56), channel_id=1, source_target_pairs={{0,2},{1,3},{2,4},{3,5},{4,6},{5,7},{6,8},{7,9},{8,10},{9,11},{10,... | collective-permute-start | bytes 688136 | tf_op jit(solution)/shard_map/ppermute | solution.py:191
  192.7 7.4 %collective-permute-start.16 = (f32[56,1024]{1,0:T(8,128)S(1)}, f32[56,1024]{1,0:T(8,128)S(1)}, u32[]{:S(2)}, u32[]{:S(2)}) collective-permute-start(f32[56,1024]{1,0:T(8,128)S(1)} %get-tuple-element.55), channel_id=1, source_target_pairs={{0,14},{1,15},{2,0},{3,1},{4,2},{5,3},{6,4},{7,5},{8,6},{9,7},{10,... | collective-permute-start | bytes 688136 | tf_op jit(solution)/shard_map/ppermute | solution.py:192
  195.3 8.4 %collective-permute-start.4 = (f32[56,768]{1,0:T(8,128)S(1)}, f32[56,768]{1,0:T(8,128)S(1)}, u32[]{:S(2)}, u32[]{:S(2)}) collective-permute-start(f32[56,768]{1,0:T(8,128)S(1)} %get-tuple-element.60), channel_id=1, source_target_pairs={{0,2},{1,3},{2,4},{3,5},{4,6},{5,7},{6,8},{7,9},{8,10},{9,11},{10,... | collective-permute-start | bytes 516104 | tf_op jit(solution)/shard_map/ppermute | solution.py:191
  198.1 7.0 %collective-permute-start.8 = (f32[56,768]{1,0:T(8,128)S(1)}, f32[56,768]{1,0:T(8,128)S(1)}, u32[]{:S(2)}, u32[]{:S(2)}) collective-permute-start(f32[56,768]{1,0:T(8,128)S(1)} %get-tuple-element.59), channel_id=1, source_target_pairs={{0,14},{1,15},{2,0},{3,1},{4,2},{5,3},{6,4},{7,5},{8,6},{9,7},{10,... | collective-permute-start | bytes 516104 | tf_op jit(solution)/shard_map/ppermute | solution.py:192
  201.2 8.0 %collective-permute-start.13 = (f32[56,1024]{1,0:T(8,128)S(1)}, f32[56,1024]{1,0:T(8,128)S(1)}, u32[]{:S(2)}, u32[]{:S(2)}) collective-permute-start(f32[56,1024]{1,0:T(8,128)S(1)} %get-tuple-element.54), channel_id=1, source_target_pairs={{0,2},{1,3},{2,4},{3,5},{4,6},{5,7},{6,8},{7,9},{8,10},{9,11},{10,... | collective-permute-start | bytes 688136 | tf_op jit(solution)/shard_map/ppermute | solution.py:191
  203.8 9.0 %collective-permute-start.17 = (f32[56,1024]{1,0:T(8,128)S(1)}, f32[56,1024]{1,0:T(8,128)S(1)}, u32[]{:S(2)}, u32[]{:S(2)}) collective-permute-start(f32[56,1024]{1,0:T(8,128)S(1)} %get-tuple-element.53), channel_id=1, source_target_pairs={{0,14},{1,15},{2,0},{3,1},{4,2},{5,3},{6,4},{7,5},{8,6},{9,7},{10,... | collective-permute-start | bytes 688136 | tf_op jit(solution)/shard_map/ppermute | solution.py:192
  206.1 9.9 %collective-permute-start.5 = (f32[56,768]{1,0:T(8,128)S(1)}, f32[56,768]{1,0:T(8,128)S(1)}, u32[]{:S(2)}, u32[]{:S(2)}) collective-permute-start(f32[56,768]{1,0:T(8,128)S(1)} %get-tuple-element.58), channel_id=1, source_target_pairs={{0,2},{1,3},{2,4},{3,5},{4,6},{5,7},{6,8},{7,9},{8,10},{9,11},{10,... | collective-permute-start | bytes 516104 | tf_op jit(solution)/shard_map/ppermute | solution.py:191
  208.6 14.1 %copy-start.4 = (f32[56,1792]{1,0:T(8,128)S(1)}, f32[56,1792]{1,0:T(8,128)}, u32[]{:S(2)}) copy-start(f32[56,1792]{1,0:T(8,128)} %param.7) | copy-start | bytes 1204228
  208.6 7.6 %collective-permute-start.9 = (f32[56,768]{1,0:T(8,128)S(1)}, f32[56,768]{1,0:T(8,128)S(1)}, u32[]{:S(2)}, u32[]{:S(2)}) collective-permute-start(f32[56,768]{1,0:T(8,128)S(1)} %get-tuple-element.57), channel_id=1, source_target_pairs={{0,14},{1,15},{2,0},{3,1},{4,2},{5,3},{6,4},{7,5},{8,6},{9,7},{10,... | collective-permute-start | bytes 516104 | tf_op jit(solution)/shard_map/ppermute | solution.py:192
  213.9 6.1 %collective-permute-start.14 = (f32[56,1024]{1,0:T(8,128)S(1)}, f32[56,1024]{1,0:T(8,128)S(1)}, u32[]{:S(2)}, u32[]{:S(2)}) collective-permute-start(f32[56,1024]{1,0:T(8,128)S(1)} %get-tuple-element.52), channel_id=1, source_target_pairs={{0,2},{1,3},{2,4},{3,5},{4,6},{5,7},{6,8},{7,9},{8,10},{9,11},{10,... | collective-permute-start | bytes 688136 | tf_op jit(solution)/shard_map/ppermute | solution.py:191
  215.7 6.0 %collective-permute-start.18 = (f32[56,1024]{1,0:T(8,128)S(1)}, f32[56,1024]{1,0:T(8,128)S(1)}, u32[]{:S(2)}, u32[]{:S(2)}) collective-permute-start(f32[56,1024]{1,0:T(8,128)S(1)} %get-tuple-element.51), channel_id=1, source_target_pairs={{0,14},{1,15},{2,0},{3,1},{4,2},{5,3},{6,4},{7,5},{8,6},{9,7},{10,... | collective-permute-start | bytes 688136 | tf_op jit(solution)/shard_map/ppermute | solution.py:192
  (3 other events, 25.0 us)
Sparse Core Ops, SparseCore 0:
  32.7 125.9 all-gather.1
